TPU v7x, 768 devices: a whole 4x8x12 slice. The times are simulated.
768 devices in a mesh: replica: 16 (over y, core), shard: 48 (over z, x).
Axes of the slice: x: 4, y: 8, z: 12, core: 2. Of those that a mesh axis runs over, the one named last changes fastest.
Arguments:
- table: bfloat16 [196608, 256], P('shard'), may hold values from -1.796875 to 1.796875
- row_state: float32 [196608], P('shard'), may hold values from 0.01 to 0.1
- touched_rows: int32 [49152], P('shard'), may hold values from 0 to 4095, as said below
- lookup_rows: int32 [16, 2304, 20], P('replica', 'shard'), may hold values from 0 to 4095, as said below
- lookup_bags: int32 [16, 2304, 20], P('replica', 'shard'), may hold values from 0 to 39
- route_counts: int32 [16, 2304], P('replica', 'shard'), may hold values from 5 to 20, as said below
- pooled_grad: float32 [30720, 256], P(('replica', 'shard')), may hold values from -6 to 6
Outputs:
- pooled: float32 [30720, 256], P(('replica', 'shard'))
- new_table: bfloat16 [196608, 256], P('shard')
- new_state: float32 [196608], P('shard')
Inputs may be any that keep to these rules, and one draw needn't show every extreme that they name: `touched_rows`: each shard's 1024 entries are distinct, and every slot's row (live or not) is listed for its owning shard d. `lookup_rows`: every entry is listed in touched_rows for the owning shard d of its pair s * 48 + d. `route_counts`: in every draw one owning shard receives 20 live slots from every sender.
All inputs are finite; a program needn't handle non-finite values.
Results may differ from a plain program's by a relative error of at most 0.004.
Values may be sent and summed in bfloat16 or wider, within the bound.
No kernel may reach another device: no remote copies, remote signals or barrier semaphores. Data moves between devices by JAX's collectives and lax.ppermute only.
A program may use at most 32 MiB of HBM per device.

v0:
```python
import jax
import jax.numpy as jnp
from jax import lax
from jax.sharding import PartitionSpec as P

learn_rate = 0.5
epsilon = 1e-08


def adagrad_rows(table, row_state, row_list, grad_rows):
    state_now = jnp.take(row_state, row_list) + jnp.mean(grad_rows * grad_rows, axis=1)
    previous = jnp.take(table, row_list, axis=0).astype(jnp.float32)
    updated = (previous - learn_rate * grad_rows / (jnp.sqrt(state_now)[:, None] + epsilon)).astype(
        jnp.bfloat16
    )
    return (updated, state_now)


def local(table, row_state, touched_rows, lookup_rows, lookup_bags, route_counts, pooled_grad):
    shards = lax.axis_size("shard")
    replicas = lax.axis_size("replica")
    capacity = lookup_rows.shape[2]
    bag_count = pooled_grad.shape[0]
    feature_width = table.shape[1]
    got_rows, got_bags, got_counts = (
        lax.all_to_all(lookup_rows, "shard", split_axis=1, concat_axis=1, tiled=True),
        lax.all_to_all(lookup_bags, "shard", split_axis=1, concat_axis=1, tiled=True),
        lax.all_to_all(route_counts, "shard", split_axis=1, concat_axis=1, tiled=True),
    )
    slot_ids = jnp.arange(capacity, dtype=jnp.int32)
    live_in = slot_ids[None, :] < got_counts[0][:, None]
    in_rows = got_rows[0]
    in_bags = got_bags[0]
    picked = jnp.take(table, in_rows.reshape(-1), axis=0).reshape(shards, capacity, feature_width)
    bag_ids = jnp.arange(bag_count, dtype=jnp.int32)
    member = ((in_bags[:, None, :] == bag_ids[None, :, None]) & live_in[:, None, :]).astype(
        jnp.bfloat16
    )
    partial_sums = jnp.einsum("sbc,sce->sbe", member, picked, preferred_element_type=jnp.float32)
    returned = lax.all_to_all(
        partial_sums.astype(jnp.bfloat16), "shard", split_axis=0, concat_axis=0, tiled=True
    ).astype(partial_sums.dtype)
    pooled = jnp.sum(returned, axis=0)
    every_grad = lax.all_gather(pooled_grad, "shard", axis=0, tiled=True)
    position = jnp.arange(shards, dtype=jnp.int32)[:, None] * bag_count + in_bags
    slot_grads = jnp.take(every_grad, position.reshape(-1), axis=0)
    hit_matrix = (
        (touched_rows[:, None] == in_rows.reshape(-1)[None, :]) & live_in.reshape(-1)[None, :]
    ).astype(jnp.float32)
    local_grad = jnp.dot(
        hit_matrix, slot_grads, precision=lax.Precision.HIGHEST, preferred_element_type=jnp.float32
    )
    mean_grad = lax.psum(local_grad, "replica") / replicas
    updated, state_now = adagrad_rows(table, row_state, touched_rows, mean_grad)
    return (pooled, table.at[touched_rows].set(updated), row_state.at[touched_rows].set(state_now))


def solution(mesh):
    return jax.shard_map(
        local,
        mesh=mesh,
        in_specs=(
            P("shard", None),
            P("shard"),
            P("shard"),
            P("replica", "shard", None),
            P("replica", "shard", None),
            P("replica", "shard"),
            P(("replica", "shard"), None),
        ),
        out_specs=(P(("replica", "shard"), None), P("shard", None), P("shard")),
        check_vma=False,
    )
```

profile of v0, /device:TPU:1, one launch (start us, length us, event | category | flops | bytes accessed | tf_op | source)
XLA Modules:
  0.0 294.5 jit_solution(7448222736881106621)
XLA Ops:
  7.3 1.6 copy.41
  8.9 0.7 copy.31
  9.6 18.8 %all-to-all-start.1 = ((s32[1,48,1]{2,0,1:T(1,128)}), s32[1,48,1]{2,0,1:T(1,128)S(1)}, u32[]{:S(2)}, u32[]{:S(2)}) async-start(s32[1,48,1]{2,0,1:T(1,128)} %copy.31), calls=%async_computation.1 | async-start | bytes 49152 | tf_op jit(solution)/shard_map/all_to_all | solution.py:28
  29.9 9.5 %all-to-all-done.1 = s32[1,48,1]{2,0,1:T(1,128)S(1)} async-done(((s32[1,48,1]{2,0,1:T(1,128)}), s32[1,48,1]{2,0,1:T(1,128)S(1)}, u32[]{:S(2)}, u32[]{:S(2)}) %all-to-all-start.1) | async-done | bytes 224 | tf_op jit(solution)/shard_map/all_to_all | solution.py:28
  39.3 4.5 %all-to-all-start.2 = ((s32[1,48,20]{2,0,1:T(1,128)}), s32[1,48,20]{2,0,1:T(1,128)S(1)}, u32[]{:S(2)}, u32[]{:S(2)}) async-start(s32[1,48,20]{2,0,1:T(1,128)} %copy.32), calls=%async_computation.2 | async-start | bytes 49152 | tf_op jit(solution)/shard_map/all_to_all | solution.py:26
  43.8 0.9 reduce
  44.9 9.8 %all-to-all-done.2 = s32[1,48,20]{2,0,1:T(1,128)S(1)} async-done(((s32[1,48,20]{2,0,1:T(1,128)}), s32[1,48,20]{2,0,1:T(1,128)S(1)}, u32[]{:S(2)}, u32[]{:S(2)}) %all-to-all-start.2) | async-done | bytes 3872 | tf_op jit(solution)/shard_map/all_to_all | solution.py:26
  54.7 4.5 %all-to-all-start = ((s32[1,48,20]{2,0,1:T(1,128)}), s32[1,48,20]{2,0,1:T(1,128)S(1)}, u32[]{:S(2)}, u32[]{:S(2)}) async-start(s32[1,48,20]{2,0,1:T(1,128)} %copy.28), calls=%async_computation | async-start | bytes 49152 | tf_op jit(solution)/shard_map/all_to_all | solution.py:27
  59.7 0.7 reduce.11
  60.6 4.1 %gather_fusion = bf16[960,256]{1,0:T(8,128)(2,1)S(1)} fusion(bf16[4096,256]{1,0:T(8,128)(2,1)S(1)} %copy.41, s32[1024]{0:T(1024)S(1)} %pad_clamp_fusion.1), kind=kCustom, calls=%fused_computation | custom fusion | bytes 986880 | tf_op jit(solution)/shard_map/jit(_take)/gather | solution.py:34
  64.9 5.1 %all-to-all-done = s32[1,48,20]{2,0,1:T(1,128)S(1)} async-done(((s32[1,48,20]{2,0,1:T(1,128)}), s32[1,48,20]{2,0,1:T(1,128)S(1)}, u32[]{:S(2)}, u32[]{:S(2)}) %all-to-all-start) | async-done | bytes 3872 | tf_op jit(solution)/shard_map/all_to_all | solution.py:27
  70.1 2.2 convolution_convert_fusion
  72.3 6.8 %all-to-all-start.3 = ((bf16[48,40,256]{2,1,0:T(8,128)(2,1)}), bf16[48,40,256]{2,1,0:T(8,128)(2,1)S(1)}, u32[]{:S(2)}, u32[]{:S(2)}) async-start(bf16[48,40,256]{2,1,0:T(8,128)(2,1)} %convolution_convert_fusion), calls=%async_computation.3 | async-start | bytes 1966080 | tf_op jit(solution)/shard_map/all_to_all | solution.py:40
  79.7 0.7 reduce.12
  80.6 56.1 %all-gather.2.cloned.1.call-done = f32[1920,256]{1,0:T(8,128)} async-done(((f32[40,256]{1,0:T(8,128)}), f32[1920,256]{1,0:T(8,128)}) %all-gather.2.cloned.1.call-update) | async-done | bytes 1966096 | tf_op jit(solution)/shard_map/all_gather | solution.py:44
  136.7 6.2 %gather_fusion.1 = f32[960,256]{1,0:T(8,128)} fusion(f32[1920,256]{1,0:T(8,128)} %all-gather.2.cloned.1.call-done, s32[1024]{0:T(1024)S(1)} %pad_clamp_fusion), kind=kCustom, calls=%fused_computation.2 | custom fusion | bytes 1969920 | tf_op jit(solution)/shard_map/jit(_take)/gather | solution.py:46
  142.9 4.4 %fusion = f32[1024,256]{1,0:T(8,128)} fusion(s32[960]{0:T(1024)S(1)} %reshape_squeeze.9, s32[1024]{0:T(1024)S(1)} %copy-done.4, pred[960]{0:T(1024)(128)(4,1)S(1)} %lt.88, f32[960,256]{1,0:T(8,128)} %gather_fusion.1, pred[960]{0:T(1024)(128)(4,1)S(1)} %compare_and_fusion.1), kind=kOutput, calls=%fused_computation.6 | convolution fusion | flops 3022110720 | bytes 2041472 | tf_op jit(solution)/shard_map/dot_general | solution.py:50
  147.4 6.2 %gather_fusion.2 = f32[1024]{0:T(1024)S(1)} fusion(f32[4096]{0:T(1024)S(1)} %copy.42, s32[1024]{0:T(1024)S(1)} %get-tuple-element.6), kind=kCustom, calls=%fused_computation.3 | custom fusion | bytes 12288 | tf_op jit(solution)/shard_map/jit(_take)/gather | solution.py:11
  153.5 0.8 convert_reduce_fusion
  154.3 116.1 %all-reduce.2.cloned.1.call-done = f32[1024,256]{1,0:T(8,128)} async-done(((f32[1024,256]{1,0:T(8,128)}), f32[1024,256]{1,0:T(8,128)}) %all-reduce.2.cloned.1.call-update) | async-done | bytes 1048592 | tf_op jit(solution)/shard_map/psum | solution.py:53
  270.4 1.4 multiply_reduce_fusion
  271.9 4.3 %scatter_fusion = f32[4096]{0:T(1024)S(1)} fusion(f32[4096]{0:T(1024)S(1)} %copy.42, s32[1024]{0:T(1024)S(1)} %get-tuple-element.7, f32[1024]{0:T(1024)S(1)} %get-tuple-element.4), kind=kCustom, calls=%fused_computation.5 | custom fusion | bytes 16384 | tf_op jit(solution)/shard_map/scatter | solution.py:55
  276.2 10.1 %scatter_custom_fusion = bf16[4096,256]{1,0:T(8,128)(2,1)S(1)} fusion(bf16[4096,256]{1,0:T(8,128)(2,1)S(1)} %copy.41, s32[1024]{0:T(1024)S(1)} %get-tuple-element.7, f32[1024,256]{1,0:T(8,128)S(1)} %copy-done.2, f32[1024]{0:T(1024)S(1)} %get-tuple-element.3, f32[]{:T(128)} %constant.68.clone.1, pred[1024]{0:T(1024)(128)(4,1)S(1)} %get-tuple-element.5, ...), kind=kCustom, calls=%fused_computation.21 | custom fusion | flops 1572864 | bytes 5252102 | tf_op jit(solution)/shard_map/scatter | solution.py:55
  286.3 1.3 copy-done.1
  (45 shorter events, 3.3 us)
Async XLA Ops:
  7.2 129.5 %all-gather.2.cloned.1.call-start = ((), (), s32[]{:S(2)}) async-start(), calls=%async_computation.4 | async-start | bytes 2007040 | tf_op jit(solution)/shard_map/all_gather | solution.py:44
  7.2 1.7 copy-start.3
  7.2 1.7 copy-start.7
  7.2 21.2 %copy-start.5 = (s32[1,48,20]{1,0,2:T(1,128)S(1)}, s32[1,48,20]{1,0,2:T(1,128)}, u32[]{:S(2)}) copy-start(s32[1,48,20]{1,0,2:T(1,128)} %param.10) | copy-start | bytes 11524
  7.2 21.9 %copy-start.6 = (s32[1,48,20]{1,0,2:T(1,128)S(1)}, s32[1,48,20]{1,0,2:T(1,128)}, u32[]{:S(2)}) copy-start(s32[1,48,20]{1,0,2:T(1,128)} %param.11) | copy-start | bytes 11524
  9.6 29.7 %all-to-all-start.1 = ((s32[1,48,1]{2,0,1:T(1,128)}), s32[1,48,1]{2,0,1:T(1,128)S(1)}, u32[]{:S(2)}, u32[]{:S(2)}) async-start(s32[1,48,1]{2,0,1:T(1,128)} %copy.31), calls=%async_computation.1 | async-start | bytes 49152 | tf_op jit(solution)/shard_map/all_to_all | solution.py:28
  39.3 15.3 %all-to-all-start.2 = ((s32[1,48,20]{2,0,1:T(1,128)}), s32[1,48,20]{2,0,1:T(1,128)S(1)}, u32[]{:S(2)}, u32[]{:S(2)}) async-start(s32[1,48,20]{2,0,1:T(1,128)} %copy.32), calls=%async_computation.2 | async-start | bytes 49152 | tf_op jit(solution)/shard_map/all_to_all | solution.py:26
  54.7 15.4 %all-to-all-start = ((s32[1,48,20]{2,0,1:T(1,128)}), s32[1,48,20]{2,0,1:T(1,128)S(1)}, u32[]{:S(2)}, u32[]{:S(2)}) async-start(s32[1,48,20]{2,0,1:T(1,128)} %copy.28), calls=%async_computation | async-start | bytes 49152 | tf_op jit(solution)/shard_map/all_to_all | solution.py:27
  72.3 81.2 %all-to-all-start.3 = ((bf16[48,40,256]{2,1,0:T(8,128)(2,1)}), bf16[48,40,256]{2,1,0:T(8,128)(2,1)S(1)}, u32[]{:S(2)}, u32[]{:S(2)}) async-start(bf16[48,40,256]{2,1,0:T(8,128)(2,1)} %convolution_convert_fusion), calls=%async_computation.3 | async-start | bytes 1966080 | tf_op jit(solution)/shard_map/all_to_all | solution.py:40
  79.0 191.4 %all-reduce.2.cloned.1.call-start = ((), (), s32[]{:S(2)}) async-start(), calls=%async_computation.5 | async-start | bytes 2097152 | tf_op jit(solution)/shard_map/psum | solution.py:53
  80.6 62.3 %copy-start.4 = (s32[1024]{0:T(1024)S(1)}, s32[1024]{0:T(1024)}, u32[]{:S(2)}) copy-start(s32[1024]{0:T(1024)} %param.9) | copy-start | bytes 12292
  271.9 4.4 %copy-start.2 = (f32[1024,256]{1,0:T(8,128)S(1)}, f32[1024,256]{1,0:T(8,128)}, u32[]{:S(2)}) copy-start(f32[1024,256]{1,0:T(8,128)} %all-reduce.2.cloned.1.call-done) | copy-start | bytes 3145732
  276.2 10.1 %copy-start = (f32[4096]{0:T(1024)}, f32[4096]{0:T(1024)S(1)}, u32[]{:S(2)}) copy-start(f32[4096]{0:T(1024)S(1)} %scatter_fusion) | copy-start | bytes 49156
  286.3 1.3 copy-start.1
Sparse Core Ops, SparseCore 0:
  11.6 125.0 all-gather.1
  147.5 122.8 all-reduce.1
where the time goes:
time: 295 us; the launch traced here: 294 us
  waiting for transfers between devices  197 us (67%)
  starting transfers between devices  34.7 us (12%)
  local copies, waits for them, and re-layouts  27.4 us (9%)
  other arithmetic  14.8 us (5%)
  between operations  14.3 us (5%)
  matrix products  6.63 us (2%)
    psum x1, waiting for transfers between devices, local(): mean_grad = lax.psum(local_grad, 'replica') / replicas  116 us
    all_gather x1, waiting for transfers between devices, local(): every_grad = lax.all_gather(pooled_grad, 'shard', axis=0, tiled=True)  56.1 us
    all_to_all x1, starting transfers between devices, local(): lax.all_to_all(route_counts, 'shard', split_axis=1, concat_axis=1, tiled=...  18.8 us
    scatter x1, other arithmetic, local(): table.at[touched_rows].set(updated)  10.1 us
    all_to_all x1, waiting for transfers between devices, local(): lax.all_to_all(lookup_rows, 'shard', split_axis=1, concat_axis=1, tiled=T...  9.82 us
    all_to_all x1, waiting for transfers between devices, local(): lax.all_to_all(route_counts, 'shard', split_axis=1, concat_axis=1, tiled=...  9.46 us
    all_to_all x1, starting transfers between devices, local(): lax.all_to_all(partial_sums.astype(jnp.bfloat16), 'shard', split_axis=0,...  6.76 us
    gather x1, local copies, waits for them, and re-layouts, local(): slot_grads = jnp.take(every_grad, position.reshape(-1), axis=0)  6.19 us
  transfers between devices with their start and end apart: 6, of which 5 were waited for; matrix products, arithmetic and copies ran while one was open for 10% of the time, Pallas kernels for 0%

commit v1 on v0

v1 whole, which is shorter than its diff:
```python
import functools

import jax
import jax.numpy as jnp
from jax import lax
from jax.experimental import pallas as pl
from jax.experimental.pallas import tpu as pltpu
from jax.sharding import PartitionSpec as P

learn_rate = 0.5
epsilon = 1e-08
bf16 = jnp.bfloat16
f32 = jnp.float32

block = 24
dead = 200
params = pltpu.CompilerParams(vmem_limit_bytes=24 * 1024 * 1024)


def iota(shape, axis):
    return lax.broadcasted_iota(jnp.int32, shape, axis)


def dot(a, b):
    return jnp.dot(a, b, preferred_element_type=f32)


def pair_of(position):
    return (position * 2731) >> 16


def slot_of(shape):
    position = iota(shape, 0)
    return position - block * pair_of(position)


def spread_matrix(shards):
    shape = (shards * block, shards)
    return jnp.where(pair_of(iota(shape, 0)) == iota(shape, 1), 1.0, 0.0)


def prep_kernel(rows_ref, bags_ref, counts_ref, grad_ref, out_ref, member_ref):
    shards, capacity = rows_ref.shape
    bag_count, width = grad_ref.shape
    flat = shards * block
    same = iota((shards, shards), 0) == iota((shards, shards), 1)
    counts = jnp.sum(
        jnp.where(same, counts_ref[...].astype(f32), 0.0), axis=1, keepdims=True
    )
    live = iota((shards, capacity), 1).astype(f32) < counts
    key = jnp.where(live, bags_ref[...], dead).astype(f32).astype(bf16)
    spread = spread_matrix(shards)
    spread_b = spread.astype(bf16)
    per_row = dot(spread_b, key)
    own = slot_of((flat, capacity)) == iota((flat, capacity), 1)
    bag = dot(jnp.where(own, per_row, 0.0).astype(bf16), jnp.ones((capacity, 128), bf16))
    match = (bag == iota((flat, 128), 1).astype(f32)) & (slot_of((flat, 128)) < capacity)
    member = jnp.where(match, 1.0, 0.0).astype(bf16)
    member_ref[...] = member
    grads = jnp.concatenate(
        [grad_ref[...], jnp.zeros((128 - bag_count, width), f32)], axis=0
    ).astype(bf16)
    rows = rows_ref[...]
    high = (rows >> 6).astype(f32).astype(bf16)
    low = (rows & 63).astype(f32).astype(bf16)
    lane = iota((capacity, width), 1)
    sub = iota((capacity, width), 0)
    meta = dot(high, jnp.where(lane == sub, 1.0, 0.0).astype(bf16)) + dot(
        low, jnp.where(lane == sub + 128, 1.0, 0.0).astype(bf16)
    )
    at_meta = jnp.where(slot_of((flat, shards)) == capacity, spread, 0.0).astype(bf16)
    out_ref[...] = (dot(member, grads) + dot(at_meta, meta.astype(bf16))).astype(bf16)


def prep(rows, bags, counts, grad):
    shards, capacity = rows.shape
    flat = shards * block
    return pl.pallas_call(
        prep_kernel,
        out_shape=(
            jax.ShapeDtypeStruct((flat, grad.shape[1]), bf16),
            jax.ShapeDtypeStruct((flat, 128), bf16),
        ),
        compiler_params=params,
        name="prep",
    )(rows, bags, counts, grad)


def hits_kernel(capacity, got_ref, listed_ref, part_ref, hits_ref):
    flat, width = got_ref.shape
    shards = flat // block
    touch = listed_ref.shape[1]
    got = got_ref[...]
    pick_shape = (shards, flat)
    pick = jnp.where(
        iota(pick_shape, 1) == block * iota(pick_shape, 0) + capacity, 1.0, 0.0
    ).astype(bf16)
    meta = dot(pick, got).astype(bf16)
    per_row = dot(spread_matrix(shards).astype(bf16), meta)
    own = (iota((flat, width), 1) & 127) == slot_of((flat, width))
    weigh = jnp.where(iota((width, 128), 0) < 128, 64.0, 1.0).astype(bf16)
    row = dot(jnp.where(own, per_row, 0.0).astype(bf16), weigh)
    row = jnp.where(slot_of((flat, 128)) < capacity, row, -1.0)
    for k in range(touch // 128):
        listed = listed_ref[:, k * 128 : (k + 1) * 128].astype(f32)
        hits_ref[:, k * 128 : (k + 1) * 128] = jnp.where(row == listed, 1.0, 0.0).astype(bf16)
    part_ref[...] = lax.dot_general(
        hits_ref[...], got, (((0,), (0,)), ((), ())), preferred_element_type=f32
    ).astype(bf16)


def find_hits(got, listed, capacity):
    flat, width = got.shape
    touch = listed.shape[1]
    return pl.pallas_call(
        functools.partial(hits_kernel, capacity),
        out_shape=(
            jax.ShapeDtypeStruct((touch, width), bf16),
            jax.ShapeDtypeStruct((flat, touch), bf16),
        ),
        compiler_params=params,
        name="hits",
    )(got, listed)


def pick_kernel(hits_ref, values_ref, out_ref):
    out_ref[...] = dot(hits_ref[...], values_ref[...]).astype(bf16)


def pick_rows(hits, values):
    return pl.pallas_call(
        pick_kernel,
        out_shape=jax.ShapeDtypeStruct((hits.shape[0], values.shape[1]), bf16),
        compiler_params=params,
        name="pick",
    )(hits, values)


def update_kernel(offset_ref, parts_ref, previous_ref, state_ref, out_ref):
    replicas, mine, width = parts_ref.shape
    grad = parts_ref[0].astype(f32)
    for k in range(1, replicas):
        grad = grad + parts_ref[k].astype(f32)
    grad = grad / replicas
    state = state_ref[...] + jnp.mean(grad * grad, axis=1, keepdims=True)
    out_ref[0:mine, :] = (
        previous_ref[...].astype(f32) - learn_rate * grad / (jnp.sqrt(state) + epsilon)
    ).astype(bf16)
    shape = (mine, width)
    at = iota(shape, 1) == iota(shape, 0) + offset_ref[0]
    line = jnp.sum(jnp.where(at, state, 0.0), axis=0, keepdims=True)
    first = line.astype(bf16).astype(f32)
    second = (line - first).astype(bf16).astype(f32)
    third = line - first - second
    sub = iota((16, width), 0)
    out_ref[mine : mine + 16, :] = jnp.where(
        sub == 0, first, jnp.where(sub == 1, second, jnp.where(sub == 2, third, 0.0))
    ).astype(bf16)


def update_rows(offset, parts, previous, state):
    _, mine, width = parts.shape
    vmem = pl.BlockSpec(memory_space=pltpu.VMEM)
    return pl.pallas_call(
        update_kernel,
        out_shape=jax.ShapeDtypeStruct((mine + 16, width), bf16),
        in_specs=[pl.BlockSpec(memory_space=pltpu.SMEM), vmem, vmem, vmem],
        compiler_params=params,
        name="update",
    )(offset, parts, previous, state)


def place_kernel(mine, every_ref, listed_ref, table_ref, state_ref, out_ref, state_out, values):
    step = pl.program_id(0)
    rows, width = table_ref.shape
    touch = listed_ref.shape[1]
    replicas = touch // mine
    stride = mine + 16

    @pl.when(step == 0)
    def _():
        for k in range(replicas):
            values[k * mine : (k + 1) * mine, :] = every_ref[k * stride : k * stride + mine, :]
        group = width // mine
        pieces = []
        for q in range(replicas // group):
            total = jnp.zeros((16, width), f32)
            for k in range(q * group, (q + 1) * group):
                total = total + every_ref[k * stride + mine : (k + 1) * stride, :].astype(f32)
            pieces.append(total)
        lines = jnp.concatenate(pieces, axis=1)
        high = state_ref.shape[0]
        listed = listed_ref[...]
        at_high = iota((high, touch), 0) == (listed >> 7)
        spread = jnp.concatenate(
            [jnp.where(at_high, lines[k : k + 1, :], 0.0) for k in range(3)], axis=0
        ).astype(bf16)
        at_low = jnp.where(iota((128, touch), 0) == (listed & 127), 1.0, 0.0).astype(bf16)
        placed = lax.dot_general(
            spread, at_low, (((1,), (1,)), ((), ())), preferred_element_type=f32
        )
        state_out[...] = state_ref[...] + (
            placed[0:high] + placed[high : 2 * high] + placed[2 * high : 3 * high]
        )

    row = (iota((rows, 128), 0) + step * rows).astype(f32)
    chosen = jnp.concatenate(
        [
            jnp.where(
                row == listed_ref[:, k * 128 : (k + 1) * 128].astype(f32), 1.0, 0.0
            ).astype(bf16)
            for k in range(touch // 128)
        ],
        axis=1,
    )
    out_ref[...] = (table_ref[...].astype(f32) + dot(chosen, values[...])).astype(bf16)


def place_rows(every, listed, table, state, mine):
    rows, width = table.shape
    touch = listed.shape[1]
    tile = 512
    high = rows // 128
    return pl.pallas_call(
        functools.partial(place_kernel, mine),
        grid=(rows // tile,),
        in_specs=[
            pl.BlockSpec(every.shape, lambda i: (0, 0)),
            pl.BlockSpec(listed.shape, lambda i: (0, 0)),
            pl.BlockSpec((tile, width), lambda i: (i, 0)),
            pl.BlockSpec((high, 128), lambda i: (0, 0)),
        ],
        out_specs=(
            pl.BlockSpec((tile, width), lambda i: (i, 0)),
            pl.BlockSpec((high, 128), lambda i: (0, 0)),
        ),
        out_shape=(
            jax.ShapeDtypeStruct((rows, width), bf16),
            jax.ShapeDtypeStruct((high, 128), f32),
        ),
        scratch_shapes=[pltpu.VMEM((touch, width), bf16)],
        compiler_params=params,
        name="place",
    )(every, listed, table, state.reshape(high, 128))


def pool_kernel(member_ref, rows_ref, out_ref):
    total = lax.dot_general(
        member_ref[...], rows_ref[...], (((0,), (0,)), ((), ())), preferred_element_type=f32
    )
    out_ref[...] = total[0 : out_ref.shape[0], :]


def pool_rows(member, rows, bag_count):
    return pl.pallas_call(
        pool_kernel,
        out_shape=jax.ShapeDtypeStruct((bag_count, rows.shape[1]), f32),
        compiler_params=params,
        name="pool",
    )(member, rows)


def local(table, row_state, touched_rows, lookup_rows, lookup_bags, route_counts, pooled_grad):
    shards = lax.axis_size("shard")
    replicas = lax.axis_size("replica")
    capacity = lookup_rows.shape[2]
    bag_count, width = pooled_grad.shape
    touch = touched_rows.shape[0]
    mine = touch // replicas
    listed = touched_rows.reshape(1, touch)

    send, member = prep(lookup_rows[0], lookup_bags[0], route_counts, pooled_grad)
    got = lax.all_to_all(
        send.reshape(shards, block, width), "shard", split_axis=0, concat_axis=0, tiled=True
    ).reshape(shards * block, width)

    replica = lax.axis_index("replica")
    values = jnp.take(table, touched_rows, axis=0, mode="clip")
    mine_values = lax.dynamic_slice(values, (replica * mine, 0), (mine, width))
    mine_rows = lax.dynamic_slice(touched_rows, (replica * mine,), (mine,))
    mine_state = jnp.take(row_state, mine_rows, mode="clip")[:, None]
    marked = jnp.zeros(row_state.shape, f32).at[touched_rows].set(
        1.0, mode="promise_in_bounds", unique_indices=True
    )
    kept_state = jnp.where(marked > 0, 0.0, row_state)
    kept_table = jnp.where(marked[:, None] > 0, jnp.zeros((), bf16), table)

    part, hits = find_hits(got, listed, capacity)
    parts = lax.all_to_all(
        part.reshape(replicas, mine, width), "replica", split_axis=0, concat_axis=0, tiled=True
    )
    picked = pick_rows(hits, values)
    offset = (lax.rem(replica, width // mine) * mine).astype(jnp.int32).reshape(1)
    updated = update_rows(offset, parts, mine_values, mine_state)
    picked, updated = lax.optimization_barrier((picked, updated))
    returned = lax.all_to_all(
        picked.reshape(shards, block, width), "shard", split_axis=0, concat_axis=0, tiled=True
    ).reshape(shards * block, width)
    every = lax.all_gather(updated, "replica", axis=0, tiled=True)
    new_table, new_state = place_rows(every, listed, kept_table, kept_state, mine)
    pooled = pool_rows(member, returned, bag_count)
    return (pooled, new_table, new_state.reshape(row_state.shape))


def solution(mesh):
    return jax.shard_map(
        local,
        mesh=mesh,
        in_specs=(
            P("shard", None),
            P("shard"),
            P("shard"),
            P("replica", "shard", None),
            P("replica", "shard", None),
            P("replica", "shard"),
            P(("replica", "shard"), None),
        ),
        out_specs=(P(("replica", "shard"), None), P("shard", None), P("shard")),
        check_vma=False,
    )
```

time: 295 us -> 116 us (0.39)
  waiting for transfers between devices: 197 us -> 9.39 us
  blocking collectives: 0 us -> 60.7 us
  starting transfers between devices: 34.7 us -> 15.4 us
  between operations: 14.3 us -> 0.75 us
  other arithmetic: 14.8 us -> 1.96 us
  local copies, waits for them, and re-layouts: 27.4 us -> 15 us
  Pallas kernels: 0 us -> 12.1 us
  matrix products: 6.63 us -> 0 us
    psum x1 -> x0, waiting for transfers between devices: 116 us -> none  [local(): mean_grad = lax.psum(local_grad, 'replica') / replicas]
    all_gather x1 -> x0, waiting for transfers between devices: 56.1 us -> none  [local(): every_grad = lax.all_gather(pooled_grad, 'shard', axis=0, tiled=True)]
    all_to_all x0 -> x1, blocking collectives: none -> 44.3 us  [local(): lax.all_to_all(send.reshape(shards, block, width), 'shard', split_axis=0,...]
    all_to_all x4 -> x2, starting transfers between devices: 34.6 us -> 15.4 us  [the longest x1 10.5 us: local(): lax.all_to_all(part.reshape(replicas, mine, width), 'replica', split_axis...]
    all_gather x0 -> x1, blocking collectives: none -> 16.4 us  [local(): every = lax.all_gather(updated, 'replica', axis=0, tiled=True)]
    all_to_all x4 -> x2, waiting for transfers between devices: 24.4 us -> 9.39 us  [the longest x1 9.39 us: local(): lax.all_to_all(part.reshape(replicas, mine, width), 'replica', split_axis...]
    pallas_call x0 -> x6, Pallas kernels: none -> 12.1 us  [the longest x1 5.33 us: place_rows(): pl.pallas_call(functools.partial(place_kernel, mine), grid=(rows // tile,...]
    gather x4 -> x2, local copies, waits for them, and re-layouts: 16.5 us -> 6.09 us  [the longest x1 5.32 us: local(): values = jnp.take(table, touched_rows, axis=0, mode='clip')]
  transfers between devices with their start and end apart: 6 -> 2, of which waited for: 5 -> 1; matrix products, arithmetic and copies ran while one was open for 10% -> 11% of each run, Pallas kernels for 0% -> 6%
where the time goes in v1:
time: 116 us; the launch traced here: 115 us
  blocking collectives  60.7 us (52%)
  starting transfers between devices  15.4 us (13%)
  local copies, waits for them, and re-layouts  15 us (13%)
  Pallas kernels  12.1 us (10%)
  waiting for transfers between devices  9.39 us (8%)
  other arithmetic  1.96 us (2%)
    all_to_all x1, blocking collectives, local(): lax.all_to_all(send.reshape(shards, block, width), 'shard', split_axis=0,...  44.3 us
    all_gather x1, blocking collectives, local(): every = lax.all_gather(updated, 'replica', axis=0, tiled=True)  16.4 us
    all_to_all x1, starting transfers between devices, local(): lax.all_to_all(part.reshape(replicas, mine, width), 'replica', split_axis...  10.5 us
    all_to_all x1, waiting for transfers between devices, local(): lax.all_to_all(part.reshape(replicas, mine, width), 'replica', split_axis...  9.39 us
    pallas_call x1, Pallas kernels, place_rows(): pl.pallas_call(functools.partial(place_kernel, mine), grid=(rows // tile,...  5.33 us
    gather x1, local copies, waits for them, and re-layouts, local(): values = jnp.take(table, touched_rows, axis=0, mode='clip')  5.32 us
    all_to_all x1, starting transfers between devices, local(): lax.all_to_all(picked.reshape(shards, block, width), 'shard', split_axis=...  4.95 us
    unnamed x16, local copies, waits for them, and re-layouts  4.42 us
  transfers between devices with their start and end apart: 2, of which 1 were waited for; matrix products, arithmetic and copies ran while one was open for 11% of the time, Pallas kernels for 6%

profile of v1, /device:TPU:1, one launch (start us, length us, event | category | flops | bytes accessed | tf_op | source)
XLA Modules:
  0.0 115.4 jit_solution(14557898648354450629)
XLA Ops:
  0.6 0.0 copy-start.4
  0.7 0.8 copy.13
  1.4 0.8 copy.14
  2.2 0.8 copy-done.2
  3.0 0.7 copy-done.5
  3.7 0.9 prep.1
  4.6 0.7 copy-done
  5.3 44.3 %all_to_all.15 = bf16[48,24,256]{2,1,0:T(8,128)(2,1)S(1)} all-to-all(bf16[48,24,256]{2,1,0:T(8,128)(2,1)S(1)} %bitcast.15), channel_id=1, replica_groups=mesh['replica'=16,'shard'=48] {'shard'}, dimensions={0} | all-to-all | bytes 1179648 | tf_op jit(solution)/shard_map/all_to_all | solution.py:273
  49.6 0.7 copy-done.3
  50.3 3.1 %hits.1 = (bf16[1024,256]{1,0:T(8,128)(2,1)}, bf16[1152,1024]{1,0:T(8,128)(2,1)S(1)}) custom-call(bf16[1152,256]{1,0:T(8,128)(2,1)S(1)} %bitcast.14, s32[1,1024]{1,0:T(1,128)S(1)} %bitcast.18), custom_call_target="tpu_custom_call" | custom-call | tf_op jit(solution)/shard_map/hits/pallas_call | solution.py:115
  53.4 10.5 %all-to-all-start.1 = ((bf16[16,64,256]{2,1,0:T(8,128)(2,1)}), bf16[16,64,256]{2,1,0:T(8,128)(2,1)S(1)}, u32[]{:S(2)}, u32[]{:S(2)}) async-start(bf16[16,64,256]{2,1,0:T(8,128)(2,1)} %bitcast.6), calls=%async_computation.1 | async-start | bytes 1048576 | tf_op jit(solution)/shard_map/all_to_all | solution.py:289
  63.9 0.1 dynamic_slice.7
  64.0 0.8 gather_fusion.1
  64.8 0.1 copy.15.state_ref
  64.9 5.3 %gather_fusion = bf16[1024,256]{1,0:T(8,128)(2,1)S(1)} fusion(bf16[4096,256]{1,0:T(8,128)(2,1)} %param.7, s32[1024]{0:T(1024)S(1)} %get-tuple-element.22), kind=kCustom, calls=%fused_computation | custom fusion | bytes 1052672 | tf_op jit(solution)/shard_map/jit(_take)/gather | solution.py:278
  70.3 1.6 %pick.1 = bf16[1152,256]{1,0:T(8,128)(2,1)} custom-call(bf16[1152,1024]{1,0:T(8,128)(2,1)S(1)} %get-tuple-element.13.hits_ref, bf16[1024,256]{1,0:T(8,128)(2,1)S(1)} %gather_fusion), custom_call_target="tpu_custom_call" | custom-call | tf_op jit(solution)/shard_map/pick/pallas_call | solution.py:131
  71.9 9.4 %all-to-all-done.1.parts_ref = bf16[16,64,256]{2,1,0:T(8,128)(2,1)S(1)} async-done(((bf16[16,64,256]{2,1,0:T(8,128)(2,1)}), bf16[16,64,256]{2,1,0:T(8,128)(2,1)S(1)}, u32[]{:S(2)}, u32[]{:S(2)}) %all-to-all-start.1) | async-done | bytes 524320 | tf_op jit(solution)/shard_map/all_to_all | solution.py:289
  81.3 0.3 update.1
  81.5 5.0 %all-to-all-start.2 = ((bf16[48,24,256]{2,1,0:T(8,128)(2,1)}), bf16[48,24,256]{2,1,0:T(8,128)(2,1)S(1)}, u32[]{:S(2)}, u32[]{:S(2)}) async-start(bf16[48,24,256]{2,1,0:T(8,128)(2,1)} %bitcast.8), calls=%async_computation.2 | async-start | bytes 1179648 | tf_op jit(solution)/shard_map/all_to_all | solution.py:296
  86.5 4.3 %scatter_custom_fusion = f32[4096]{0:T(1024)S(1)} fusion(s32[1024]{0:T(1024)S(1)} %get-tuple-element.21, f32[1024]{0:T(1024)S(1)} %broadcast.7, f32[]{:T(128)} %constant.6.clone.1), kind=kCustom, calls=%fused_computation.7 | custom fusion | bytes 16388 | tf_op jit(solution)/shard_map/scatter | solution.py:282
  90.8 1.9 %broadcast_select_fusion.table_ref = bf16[4096,256]{1,0:T(8,128)(2,1)S(1)} fusion(bf16[4096,256]{1,0:T(8,128)(2,1)} %param.7, pred[4096]{0:T(1024)(128)(4,1)S(1)} %get-tuple-element.20), kind=kLoop, calls=%fused_computation.3 | loop fusion | flops 1048576 | bytes 4198400 | tf_op jit(solution)/shard_map/jit(_where)/select_n | solution.py:286
  92.8 16.4 %all_gather.3.every_ref = bf16[1280,256]{1,0:T(8,128)(2,1)S(1)} all-gather(bf16[80,256]{1,0:T(8,128)(2,1)S(1)} %update.1), channel_id=1, replica_groups=mesh['replica'=16,'shard'=48] {'replica'}, dimensions={0}, use_global_device_ids=true | all-gather | bytes 696320 | tf_op jit(solution)/shard_map/all_gather | solution.py:299
  109.2 5.3 %place.1 = (bf16[4096,256]{1,0:T(8,128)(2,1)}, f32[32,128]{1,0:T(8,128)}) custom-call(bf16[1280,256]{1,0:T(8,128)(2,1)S(1)} %all_gather.3.every_ref, s32[1,1024]{1,0:T(1,128)S(1)} %bitcast.19, bf16[4096,256]{1,0:T(8,128)(2,1)S(1)} %broadcast_select_fusion.table_ref, f32[32,128]{1,0:T(8,128)S(1)} %get-tuple-element.19.state_ref), custom_call_target="tpu_custom_call" | custom-call | tf_op jit(solution)/shard_map/place/pallas_call | solution.py:224
  114.5 0.9 pool.1
  (15 shorter events, 0.1 us)
Async XLA Ops:
  0.6 63.3 %copy-start.4 = (s32[1024]{0:T(1024)S(1)}, s32[1024]{0:T(1024)}, u32[]{:S(2)}) copy-start(s32[1024]{0:T(1024)} %param.9) | copy-start | bytes 12292
  0.6 63.4 %copy-start.6 = (f32[4096]{0:T(1024)S(1)}, f32[4096]{0:T(1024)}, u32[]{:S(2)}) copy-start(f32[4096]{0:T(1024)} %param.8) | copy-start | bytes 49156
  2.2 0.8 copy-start.2
  3.0 0.7 copy-start.5
  4.6 0.7 copy-start
  49.6 0.7 copy-start.3
  53.4 27.8 %all-to-all-start.1 = ((bf16[16,64,256]{2,1,0:T(8,128)(2,1)}), bf16[16,64,256]{2,1,0:T(8,128)(2,1)S(1)}, u32[]{:S(2)}, u32[]{:S(2)}) async-start(bf16[16,64,256]{2,1,0:T(8,128)(2,1)} %bitcast.6), calls=%async_computation.1 | async-start | bytes 1048576 | tf_op jit(solution)/shard_map/all_to_all | solution.py:289
  81.5 33.0 %all-to-all-start.2 = ((bf16[48,24,256]{2,1,0:T(8,128)(2,1)}), bf16[48,24,256]{2,1,0:T(8,128)(2,1)S(1)}, u32[]{:S(2)}, u32[]{:S(2)}) async-start(bf16[48,24,256]{2,1,0:T(8,128)(2,1)} %bitcast.8), calls=%async_computation.2 | async-start | bytes 1179648 | tf_op jit(solution)/shard_map/all_to_all | solution.py:296
  92.8 21.7 %copy-start.1 = (bf16[1152,128]{1,0:T(8,128)(2,1)S(1)}, bf16[1152,128]{1,0:T(8,128)(2,1)}, u32[]{:S(2)}) copy-start(bf16[1152,128]{1,0:T(8,128)(2,1)} %copy-done) | copy-start | bytes 884740

commit v2 on v1

v2 whole, which is shorter than its diff:
```python
import functools

import jax
import jax.numpy as jnp
from jax import lax
from jax.experimental import pallas as pl
from jax.experimental.pallas import tpu as pltpu
from jax.sharding import PartitionSpec as P

learn_rate = 0.5
epsilon = 1e-08
bf16 = jnp.bfloat16
f32 = jnp.float32

block = 24
dead = 200
large = pltpu.CompilerParams(vmem_limit_bytes=60 * 1024 * 1024)
params = pltpu.CompilerParams(vmem_limit_bytes=24 * 1024 * 1024)


def iota(shape, axis):
    return lax.broadcasted_iota(jnp.int32, shape, axis)


def dot(a, b):
    return jnp.dot(a, b, preferred_element_type=f32)


def pair_of(position):
    return (position * 2731) >> 16


def slot_of(shape):
    position = iota(shape, 0)
    return position - block * pair_of(position)


def spread_matrix(shards):
    shape = (shards * block, shards)
    return jnp.where(pair_of(iota(shape, 0)) == iota(shape, 1), 1.0, 0.0)


def keys_of(bags_ref, counts_ref):
    capacity, _, shards = bags_ref.shape
    bags = bags_ref[...].reshape(capacity, shards)
    live = iota((capacity, shards), 0) < counts_ref[...]
    return jnp.where(live, bags, dead).astype(f32).astype(bf16)


def dot_nt(a, b):
    return lax.dot_general(a, b, (((1,), (1,)), ((), ())), preferred_element_type=f32)


def dot_tn(a, b):
    return lax.dot_general(a, b, (((0,), (0,)), ((), ())), preferred_element_type=f32)


def prep_kernel(rows_ref, bags_ref, counts_ref, grad_ref, out_ref, held, sems):
    capacity, _, shards = rows_ref.shape
    bag_count, width = grad_ref.shape
    flat = shards * block
    key = keys_of(bags_ref, counts_ref)
    spread = spread_matrix(shards)
    per_row = dot_nt(spread.astype(bf16), key)
    own = slot_of((flat, capacity)) == iota((flat, capacity), 1)
    bag = dot(jnp.where(own, per_row, 0.0).astype(bf16), jnp.ones((capacity, 128), bf16))
    match = (bag == iota((flat, 128), 1).astype(f32)) & (slot_of((flat, 128)) < capacity)
    member = jnp.where(match, 1.0, 0.0).astype(bf16)
    grads = jnp.concatenate(
        [grad_ref[...], jnp.zeros((128 - bag_count, width), f32)], axis=0
    ).astype(bf16)
    rows = rows_ref[...].reshape(capacity, shards)
    high = (rows >> 6).astype(f32).astype(bf16)
    low = (rows & 63).astype(f32).astype(bf16)
    lane = iota((width, capacity), 0)
    sub = iota((width, capacity), 1)
    meta = dot(jnp.where(lane == sub, 1.0, 0.0).astype(bf16), high) + dot(
        jnp.where(lane == sub + 128, 1.0, 0.0).astype(bf16), low
    )
    at_meta = jnp.where(slot_of((flat, shards)) == capacity, spread, 0.0).astype(bf16)
    meta = meta.astype(bf16)
    pieces = sems.shape[0]
    size = flat // pieces
    copies = []
    for k in range(pieces):
        here = slice(k * size, (k + 1) * size)
        held[here, :] = (dot(member[here], grads) + dot_nt(at_meta[here], meta)).astype(bf16)
        at = pl.ds(k * size, size)
        copies.append(pltpu.make_async_copy(held.at[at], out_ref.at[at], sems.at[k]))
        copies[-1].start()
    for copy in copies:
        copy.wait()


def prep(rows, bags, counts, grad):
    shards = rows.shape[2]
    return pl.pallas_call(
        prep_kernel,
        out_shape=jax.ShapeDtypeStruct((shards * block, grad.shape[1]), bf16),
        out_specs=pl.BlockSpec(memory_space=pltpu.HBM),
        scratch_shapes=[
            pltpu.VMEM((shards * block, grad.shape[1]), bf16),
            pltpu.SemaphoreType.DMA((4,)),
        ],
        compiler_params=large,
        name="prep",
    )(rows, bags, counts, grad)


def packed_slot(position, capacity):
    whole = 16
    rest = capacity - whole
    tail = position - 2 * whole
    right = ((position >= whole) & (position < 2 * whole)) | (tail >= rest)
    slot = jnp.where(
        position < 2 * whole,
        position & (whole - 1),
        whole + jnp.where(tail >= rest, tail - rest, tail),
    )
    return slot, right


def member_kernel(bags_ref, counts_ref, out_ref):
    capacity, _, shards = bags_ref.shape
    pack = 2 * capacity
    flat = shards * pack
    key = keys_of(bags_ref, counts_ref)

    def pair_and_place(shape):
        row = iota(shape, 0)
        pair = (row * 13108) >> 19
        return pair, row - pack * pair

    shape = (flat, shards)
    spread = jnp.where(pair_and_place(shape)[0] == iota(shape, 1), 1.0, 0.0).astype(bf16)
    per_row = dot_nt(spread, key)
    shape = (flat, capacity)
    slot, _ = packed_slot(pair_and_place(shape)[1], capacity)
    own = jnp.where(slot == iota(shape, 1), per_row, 0.0).astype(bf16)
    bag = dot(own, jnp.ones((capacity, 128), bf16))
    shape = (flat, 128)
    _, right = packed_slot(pair_and_place(shape)[1], capacity)
    bag = bag + jnp.where(right, 64.0, 0.0)
    out_ref[...] = jnp.where(bag == iota(shape, 1).astype(f32), 1.0, 0.0).astype(bf16)


def member_matrix(bags, counts):
    capacity, _, shards = bags.shape
    return pl.pallas_call(
        member_kernel,
        out_shape=jax.ShapeDtypeStruct((shards * 2 * capacity, 128), bf16),
        compiler_params=params,
        name="member",
    )(bags, counts)


def sort_kernel(line_ref, column_ref, line_out):
    touch = line_ref.shape[1]
    tiles = touch // 128
    column = jnp.broadcast_to(column_ref[...], (touch, 128))
    lanes = iota((touch, 128), 1).astype(f32)
    below = jnp.zeros((touch, 128), f32)
    for k in range(tiles):
        line = line_ref[:, k * 128 : (k + 1) * 128]
        below = below + jnp.where(line < column, 1.0, 0.0)
    rank_column = jnp.sum(below, axis=1, keepdims=True)
    for k in range(tiles):
        at = rank_column == lanes + 128.0 * k
        line_out[:, k * 128 : (k + 1) * 128] = jnp.sum(
            jnp.where(at, column, 0.0), axis=0, keepdims=True
        ).astype(jnp.int32)


def sort_list(touched):
    touch = touched.shape[0]
    values = touched.astype(f32)
    return pl.pallas_call(
        sort_kernel,
        out_shape=jax.ShapeDtypeStruct((1, touch), jnp.int32),
        compiler_params=params,
        name="sort",
    )(values.reshape(1, touch), values.reshape(touch, 1))


def hit_matrix(got_ref, column_ref, hits, capacity):
    flat, width = got_ref.shape
    shards = flat // block
    column = column_ref[...]
    got = got_ref[...]
    meta = got.astype(f32).reshape(shards, block, width)[:, capacity : capacity + 1, :]
    shape = (shards, block, width)
    own = (iota(shape, 2) & 127) == iota(shape, 1)
    spread = jnp.where(own, jnp.broadcast_to(meta, shape), 0.0).reshape(flat, width).astype(bf16)
    weigh = jnp.where(iota((8, width), 1) < 128, 64.0, 1.0).astype(bf16)
    rows = dot_nt(weigh, spread)
    lane = iota((8, flat), 1)
    rows = jnp.where(lane - block * pair_of(lane) < capacity, rows, -1.0)
    for k in range(flat // 128):
        line = rows[0:1, k * 128 : (k + 1) * 128]
        hits[:, k * 128 : (k + 1) * 128] = jnp.where(column == line, 1.0, 0.0).astype(bf16)
    return got


def hits_kernel(capacity, got_ref, column_ref, hits_ref):
    hit_matrix(got_ref, column_ref, hits_ref, capacity)


def find_hits(got, column, capacity):
    flat, width = got.shape
    touch = column.shape[0]
    return pl.pallas_call(
        functools.partial(hits_kernel, capacity),
        out_shape=jax.ShapeDtypeStruct((touch, flat), bf16),
        compiler_params=params,
        name="hits",
    )(got, column)


def pick_kernel(hits, values_ref, out_ref):
    shards, pack, half = out_ref.shape
    whole = 16
    rest = pack // 2 - whole
    rows = dot_tn(hits[...], values_ref[...]).reshape(shards, block, 2 * half)
    left, right = rows[:, :, 0:half], rows[:, :, half : 2 * half]
    first = iota((shards, block - whole, half), 1) < rest
    mixed = jnp.where(
        first, left[:, whole:block, :], pltpu.roll(right[:, whole:block, :], rest, 1)
    )
    out_ref[...] = jnp.concatenate(
        [left[:, 0:whole, :], right[:, 0:whole, :], mixed], axis=1
    ).astype(bf16)


def pick_rows(hits, values, shards, capacity):
    return pl.pallas_call(
        pick_kernel,
        out_shape=jax.ShapeDtypeStruct((shards, 2 * capacity, values.shape[1] // 2), bf16),
        compiler_params=params,
        name="pick",
    )(hits, values)


def update_kernel(offset_ref, parts_ref, previous_ref, state_ref, out_ref):
    replicas, mine, width = parts_ref.shape
    grad = parts_ref[0].astype(f32)
    for k in range(1, replicas):
        grad = grad + parts_ref[k].astype(f32)
    grad = grad / replicas
    state = state_ref[...] + jnp.mean(grad * grad, axis=1, keepdims=True)
    out_ref[0:mine, :] = (
        previous_ref[...].astype(f32) - learn_rate * grad / (jnp.sqrt(state) + epsilon)
    ).astype(bf16)
    shape = (mine, width)
    at = iota(shape, 1) == iota(shape, 0) + offset_ref[0]
    line = jnp.sum(jnp.where(at, state, 0.0), axis=0, keepdims=True)
    first = line.astype(bf16).astype(f32)
    second = (line - first).astype(bf16).astype(f32)
    third = line - first - second
    sub = iota((16, width), 0)
    out_ref[mine : mine + 16, :] = jnp.where(
        sub == 0, first, jnp.where(sub == 1, second, jnp.where(sub == 2, third, 0.0))
    ).astype(bf16)


def update_rows(offset, parts, previous, state):
    _, mine, width = parts.shape
    vmem = pl.BlockSpec(memory_space=pltpu.VMEM)
    return pl.pallas_call(
        update_kernel,
        out_shape=jax.ShapeDtypeStruct((mine + 16, width), bf16),
        in_specs=[pl.BlockSpec(memory_space=pltpu.SMEM), vmem, vmem, vmem],
        compiler_params=params,
        name="update",
    )(offset, parts, previous, state)


def place_kernel(
    mine, starts, every_ref, listed_ref, tiles_ref, table_ref, state_ref, out_ref, state_out, values
):
    step = pl.program_id(0)
    rows, width = table_ref.shape
    touch = listed_ref.shape[1]
    replicas = touch // mine
    stride = mine + 16

    @pl.when(step == 0)
    def _():
        values[touch:, :] = jnp.zeros((256, width), bf16)
        for k in range(replicas):
            values[k * mine : (k + 1) * mine, :] = every_ref[k * stride : k * stride + mine, :]
        group = width // mine
        pieces = []
        for q in range(replicas // group):
            lines = jnp.zeros((16, width), f32)
            for k in range(q * group, (q + 1) * group):
                lines = lines + every_ref[k * stride + mine : (k + 1) * stride, :].astype(f32)
            pieces.append(lines)
        lines = jnp.concatenate(pieces, axis=1)
        high = state_ref.shape[0]
        listed = listed_ref[...]
        at_high = iota((high, touch), 0) == (listed >> 7)
        spread = jnp.concatenate(
            [jnp.where(at_high, lines[k : k + 1, :], 0.0) for k in range(3)], axis=0
        ).astype(bf16)
        at_low = jnp.where(iota((128, touch), 0) == (listed & 127), 1.0, 0.0).astype(bf16)
        placed = dot_nt(spread, at_low)
        state_out[...] = state_ref[...] + (
            placed[0:high] + placed[high : 2 * high] + placed[2 * high : 3 * high]
        )

    for k in range(rows // 128):
        at = step * (rows // 128) + k
        tile = starts[at] >> 7
        row = iota((128, 128), 0) + at * 128
        chosen = jnp.concatenate(
            [
                jnp.where(row == tiles_ref[pl.ds(tile + n, 1), :], 1.0, 0.0).astype(bf16)
                for n in range(2)
            ],
            axis=1,
        )
        window = values[pl.ds(pl.multiple_of(tile * 128, 128), 256), :]
        here = slice(k * 128, (k + 1) * 128)
        out_ref[here, :] = (table_ref[here, :].astype(f32) + dot(chosen, window)).astype(bf16)


def place_rows(starts, every, listed, table, state, mine, tile):
    rows, width = table.shape
    touch = listed.shape[1]
    high = rows // 128
    tiles = jnp.pad(listed.reshape(touch // 128, 128), ((0, 8), (0, 0)), constant_values=-1)
    whole = lambda i, starts: (0, 0)
    return pl.pallas_call(
        functools.partial(place_kernel, mine),
        grid_spec=pltpu.PrefetchScalarGridSpec(
            num_scalar_prefetch=1,
            grid=(rows // tile,),
            in_specs=[
                pl.BlockSpec(every.shape, whole),
                pl.BlockSpec(listed.shape, whole),
                pl.BlockSpec(tiles.shape, whole),
                pl.BlockSpec((tile, width), lambda i, starts: (i, 0)),
                pl.BlockSpec((high, 128), whole),
            ],
            out_specs=(
                pl.BlockSpec((tile, width), lambda i, starts: (i, 0)),
                pl.BlockSpec((high, 128), whole),
            ),
            scratch_shapes=[pltpu.VMEM((touch + 256, width), bf16)],
        ),
        out_shape=(
            jax.ShapeDtypeStruct((rows, width), bf16),
            jax.ShapeDtypeStruct((high, 128), f32),
        ),
        compiler_params=params,
        name="place",
    )(starts, every, listed, tiles, table, state.reshape(high, 128))


def pool_kernel(member_ref, rows_ref, out_ref):
    shards, pack, half = rows_ref.shape
    bag_count = out_ref.shape[0]
    rows = rows_ref[...].astype(f32).reshape(shards * pack, half).astype(bf16)
    total = dot_tn(member_ref[...], rows)
    out_ref[...] = jnp.concatenate([total[0:bag_count], total[64 : 64 + bag_count]], axis=1)


def pool_rows(member, rows, bag_count):
    return pl.pallas_call(
        pool_kernel,
        out_shape=jax.ShapeDtypeStruct((bag_count, 2 * rows.shape[2]), f32),
        compiler_params=params,
        name="pool",
    )(member, rows)


def local(table, row_state, touched_rows, lookup_rows, lookup_bags, route_counts, pooled_grad):
    shards = lax.axis_size("shard")
    replicas = lax.axis_size("replica")
    capacity = lookup_rows.shape[2]
    bag_count, width = pooled_grad.shape
    touch = touched_rows.shape[0]
    mine = touch // replicas
    rows = row_state.shape[0]
    tile = 1024

    bags = jnp.transpose(lookup_bags, (2, 0, 1))
    send = prep(jnp.transpose(lookup_rows, (2, 0, 1)), bags, route_counts, pooled_grad)
    got = lax.all_to_all(
        send.reshape(shards, block, width), "shard", split_axis=0, concat_axis=0, tiled=True
    ).reshape(shards * block, width)

    listed = sort_list(touched_rows)
    column = jnp.broadcast_to(listed.reshape(touch, 1).astype(f32), (touch, 128))
    order = listed.reshape(touch)
    bounds = jnp.arange(rows // 128, dtype=jnp.int32) * 128
    starts = jnp.sum((touched_rows[None, :] < bounds[:, None]).astype(jnp.int32), axis=1)
    replica = lax.axis_index("replica")
    values = jnp.take(table, order, axis=0, mode="clip")
    mine_values = lax.dynamic_slice(values, (replica * mine, 0), (mine, width))
    mine_rows = lax.dynamic_slice(order, (replica * mine,), (mine,))
    mine_state = jnp.take(row_state, mine_rows, mode="clip")[:, None]
    marked = jnp.zeros(row_state.shape, f32).at[touched_rows].set(
        1.0, mode="promise_in_bounds", unique_indices=True
    )
    kept_state = jnp.where(marked > 0, 0.0, row_state)
    kept_table = jnp.where(marked[:, None] > 0, jnp.zeros((), bf16), table)
    got, column, kept_state, kept_table, mine_state, mine_values, starts = (
        lax.optimization_barrier(
            (got, column, kept_state, kept_table, mine_state, mine_values, starts)
        )
    )

    hits = find_hits(got, column, capacity)
    part = dot(hits, got).astype(bf16)
    parts = lax.all_to_all(
        part.reshape(replicas, mine, width), "replica", split_axis=0, concat_axis=0, tiled=True
    )
    picked = pick_rows(hits, values, shards, capacity)
    member = member_matrix(bags, route_counts)
    offset = (lax.rem(replica, width // mine) * mine).astype(jnp.int32).reshape(1)
    updated = update_rows(offset, parts, mine_values, mine_state)
    picked, member, updated = lax.optimization_barrier((picked, member, updated))
    returned = lax.all_to_all(picked, "shard", split_axis=0, concat_axis=0, tiled=True)
    every = lax.all_gather(updated, "replica", axis=0, tiled=True)
    new_table, new_state = place_rows(starts, every, listed, kept_table, kept_state, mine, tile)
    pooled = pool_rows(member, returned, bag_count)
    return (pooled, new_table, new_state.reshape(row_state.shape))


def solution(mesh):
    return jax.shard_map(
        local,
        mesh=mesh,
        in_specs=(
            P("shard", None),
            P("shard"),
            P("shard"),
            P("replica", "shard", None),
            P("replica", "shard", None),
            P("replica", "shard"),
            P(("replica", "shard"), None),
        ),
        out_specs=(P(("replica", "shard"), None), P("shard", None), P("shard")),
        check_vma=False,
    )
```

time: 116 us -> 109 us (0.940)
  blocking collectives: 60.7 us -> 16.3 us
  waiting for transfers between devices: 9.39 us -> 30.9 us
  starting transfers between devices: 15.4 us -> 34.5 us
  local copies, waits for them, and re-layouts: 15 us -> 11.2 us
  matrix products: 0 us -> 1.64 us
  Pallas kernels: 12.1 us -> 10.9 us
    all_to_all x1 -> x0, blocking collectives: 44.3 us -> none  [local(): lax.all_to_all(send.reshape(shards, block, width), 'shard', split_axis=0,...]
    all_to_all x1 -> x2, starting transfers between devices: 4.95 us -> 23.9 us  [the longest x1 18.8 us: local(): lax.all_to_all(send.reshape(shards, block, width), 'shard', split_axis=0,...]
    all_to_all x1 -> x2, waiting for transfers between devices: 0.01 us -> 17 us  [the longest x1 12.5 us: local(): lax.all_to_all(send.reshape(shards, block, width), 'shard', split_axis=0,...]
    all_to_all x1, waiting for transfers between devices: 9.39 us -> 13.9 us  [local(): lax.all_to_all(part.reshape(replicas, mine, width), 'replica', split_axis...]
    unnamed x16 -> x18, local copies, waits for them, and re-layouts: 4.42 us -> 1.59 us
    dot_general x0 -> x1, matrix products: none -> 1.64 us  [dot(): return jnp.dot(a, b, preferred_element_type=f32)]
    gather x1, local copies, waits for them, and re-layouts: 5.32 us -> 3.94 us  [local(): values = jnp.take(table, order, axis=0, mode='clip')]
    pallas_call x5 -> x7, Pallas kernels: 11.9 us -> 10.6 us  [the longest x1 3.41 us: place_rows(): pl.pallas_call(functools.partial(place_kernel, mine), grid_spec=pltpu.Pre...]
  transfers between devices with their start and end apart: 2 -> 3, of which waited for: 1 -> 3; matrix products, arithmetic and copies ran while one was open for 11% -> 11% of each run, Pallas kernels for 6% -> 6%
where the time goes in v2:
time: 109 us
  starting transfers between devices  34.5 us (32%)
  waiting for transfers between devices  30.9 us (28%)
  blocking collectives  16.3 us (15%)
  local copies, waits for them, and re-layouts  11.2 us (10%)
  Pallas kernels  10.9 us (10%)
  other arithmetic  2.66 us (2%)
  matrix products  1.64 us (2%)
    all_to_all x1, starting transfers between devices, local(): lax.all_to_all(send.reshape(shards, block, width), 'shard', split_axis=0,...  18.8 us
    all_gather x1, blocking collectives, local(): every = lax.all_gather(updated, 'replica', axis=0, tiled=True)  16.3 us
    all_to_all x1, waiting for transfers between devices, local(): lax.all_to_all(part.reshape(replicas, mine, width), 'replica', split_axis...  13.9 us
    all_to_all x1, waiting for transfers between devices, local(): lax.all_to_all(send.reshape(shards, block, width), 'shard', split_axis=0,...  12.5 us
    all_to_all x1, starting transfers between devices, local(): lax.all_to_all(part.reshape(replicas, mine, width), 'replica', split_axis...  10.6 us
    all_to_all x1, starting transfers between devices, local(): lax.all_to_all(picked, 'shard', split_axis=0, concat_axis=0, tiled=True)  5.09 us
    all_to_all x1, waiting for transfers between devices, local(): lax.all_to_all(picked, 'shard', split_axis=0, concat_axis=0, tiled=True)  4.56 us
    scatter x1, local copies, waits for them, and re-layouts, local(): jnp.zeros(row_state.shape, f32).at[touched_rows]  4.32 us
  transfers between devices with their start and end apart: 3, of which 3 were waited for; matrix products, arithmetic and copies ran while one was open for 11% of the time, Pallas kernels for 6%

profile of v2, /device:TPU:1, one launch (start us, length us, event | category | flops | bytes accessed | tf_op | source)
XLA Modules:
  0.0 108.9 jit_solution(17867823002017123714)
XLA Ops:
  0.6 2.6 %prep.1 = bf16[1152,256]{1,0:T(8,128)(2,1)} custom-call(s32[20,1,48]{2,1,0:T(1,128)} %bitcast.30, s32[20,1,48]{2,1,0:T(1,128)} %bitcast.23, s32[1,48]{1,0:T(1,128)} %counts_ref.3, f32[40,256]{1,0:T(8,128)} %grad_ref.1), custom_call_target="tpu_custom_call" | custom-call | tf_op jit(solution)/shard_map/prep/pallas_call | solution.py:97
  3.3 18.8 %all-to-all-start = ((bf16[48,24,256]{2,1,0:T(8,128)(2,1)}), bf16[48,24,256]{2,1,0:T(8,128)(2,1)S(1)}, u32[]{:S(2)}, u32[]{:S(2)}) async-start(bf16[48,24,256]{2,1,0:T(8,128)(2,1)} %bitcast.27), calls=%async_computation | async-start | bytes 1179648 | tf_op jit(solution)/shard_map/all_to_all | solution.py:389
  22.1 0.8 compare_select_fusion
  22.9 0.2 copy.13.column_ref
  23.1 1.0 sort.1.listed_ref
  24.3 3.9 %gather_fusion.1 = bf16[1024,256]{1,0:T(8,128)(2,1)S(1)} fusion(bf16[4096,256]{1,0:T(8,128)(2,1)S(1)} %copy-done.6, s32[1024]{0:T(1024)S(1)} %broadcast_clamp_fusion), kind=kCustom, calls=%fused_computation.1 | custom fusion | bytes 1052672 | tf_op jit(solution)/shard_map/jit(_take)/gather | solution.py:399
  28.3 0.8 gather_fusion
  29.0 4.3 %scatter_custom_fusion = f32[4096]{0:T(1024)S(1)} fusion(s32[1024]{0:T(1024)S(1)} %get-tuple-element.29, f32[1024]{0:T(1024)S(1)} %broadcast.14, f32[]{:T(128)} %constant.12.clone.1), kind=kCustom, calls=%fused_computation.9 | custom fusion | bytes 16388 | tf_op jit(solution)/shard_map/scatter | solution.py:403
  33.6 1.7 %broadcast_select_fusion.table_ref = bf16[4096,256]{1,0:T(8,128)(2,1)} fusion(bf16[4096,256]{1,0:T(8,128)(2,1)S(1)} %copy-done.6, pred[4096]{0:T(1024)(128)(4,1)S(1)} %get-tuple-element.28), kind=kLoop, calls=%fused_computation.3 | loop fusion | flops 1048576 | bytes 4198400 | tf_op jit(solution)/shard_map/jit(_where)/select_n | solution.py:407
  35.3 12.5 %all-to-all-done = bf16[48,24,256]{2,1,0:T(8,128)(2,1)S(1)} async-done(((bf16[48,24,256]{2,1,0:T(8,128)(2,1)}), bf16[48,24,256]{2,1,0:T(8,128)(2,1)S(1)}, u32[]{:S(2)}, u32[]{:S(2)}) %all-to-all-start) | async-done | bytes 589856 | tf_op jit(solution)/shard_map/all_to_all | solution.py:389
  48.0 0.8 hits.1
  48.8 1.6 %convolution_convert_fusion = bf16[1024,256]{1,0:T(8,128)(2,1)} fusion(bf16[1024,1152]{1,0:T(8,128)(2,1)S(1)} %hits.1, bf16[1152,256]{1,0:T(8,128)(2,1)S(1)} %bitcast.19), kind=kOutput, calls=%fused_computation.4 | convolution fusion | flops 604241920 | bytes 3473408 | tf_op jit(solution)/shard_map/dot_general | solution.py:26
  50.4 10.6 %all-to-all-start.1 = ((bf16[16,64,256]{2,1,0:T(8,128)(2,1)}), bf16[16,64,256]{2,1,0:T(8,128)(2,1)S(1)}, u32[]{:S(2)}, u32[]{:S(2)}) async-start(bf16[16,64,256]{2,1,0:T(8,128)(2,1)} %bitcast.28), calls=%async_computation.1 | async-start | bytes 1048576 | tf_op jit(solution)/shard_map/all_to_all | solution.py:416
  61.0 0.9 member.1.member_ref
  62.0 0.8 copy-done.2
  62.8 0.8 pick.1
  63.6 0.8 copy-done.1
  64.5 13.9 %all-to-all-done.1.parts_ref = bf16[16,64,256]{2,1,0:T(8,128)(2,1)S(1)} async-done(((bf16[16,64,256]{2,1,0:T(8,128)(2,1)}), bf16[16,64,256]{2,1,0:T(8,128)(2,1)S(1)}, u32[]{:S(2)}, u32[]{:S(2)}) %all-to-all-start.1) | async-done | bytes 524320 | tf_op jit(solution)/shard_map/all_to_all | solution.py:416
  78.3 0.3 update.1
  78.6 5.1 %all-to-all-start.2 = ((bf16[48,40,128]{2,1,0:T(8,128)(2,1)}), bf16[48,40,128]{2,1,0:T(8,128)(2,1)S(1)}, u32[]{:S(2)}, u32[]{:S(2)}) async-start(bf16[48,40,128]{2,1,0:T(8,128)(2,1)} %copy-done.1), calls=%async_computation.2 | async-start | bytes 983040 | tf_op jit(solution)/shard_map/all_to_all | solution.py:424
  83.7 16.3 %all_gather.3.every_ref = bf16[1280,256]{1,0:T(8,128)(2,1)S(1)} all-gather(bf16[80,256]{1,0:T(8,128)(2,1)S(1)} %update.1), channel_id=1, replica_groups=mesh['replica'=16,'shard'=48] {'replica'}, dimensions={0}, use_global_device_ids=true | all-gather | bytes 696320 | tf_op jit(solution)/shard_map/all_gather | solution.py:425
  100.0 3.4 %place.1 = (bf16[4096,256]{1,0:T(8,128)(2,1)}, f32[32,128]{1,0:T(8,128)}) custom-call(s32[32]{0:T(128)S(1)} %convert_reduce_fusion.starts, bf16[1280,256]{1,0:T(8,128)(2,1)S(1)} %all_gather.3.every_ref, s32[1,1024]{1,0:T(1,128)S(1)} %sort.1.listed_ref, s32[16,128]{1,0:T(8,128)S(1)} %pad.4.tiles_ref, bf16[4096,256]{1,0:T(8,128)(2,1)S(1)} %copy-done, ...), custom_call_target="tpu_custom_call" | custom-call | tf_op jit(solution)/shard_map/place/pallas_call | solution.py:333
  103.4 4.6 %all-to-all-done.2.rows_ref = bf16[48,40,128]{2,1,0:T(8,128)(2,1)S(1)} async-done(((bf16[48,40,128]{2,1,0:T(8,128)(2,1)}), bf16[48,40,128]{2,1,0:T(8,128)(2,1)S(1)}, u32[]{:S(2)}, u32[]{:S(2)}) %all-to-all-start.2) | async-done | bytes 491552 | tf_op jit(solution)/shard_map/all_to_all | solution.py:424
  108.0 0.9 pool.1
  (28 shorter events, 0.6 us)
Async XLA Ops:
  0.6 23.6 %copy-start.6 = (bf16[4096,256]{1,0:T(8,128)(2,1)S(1)}, bf16[4096,256]{1,0:T(8,128)(2,1)}, u32[]{:S(2)}) copy-start(bf16[4096,256]{1,0:T(8,128)(2,1)} %param.7) | copy-start | bytes 6291460
  3.3 44.5 %all-to-all-start = ((bf16[48,24,256]{2,1,0:T(8,128)(2,1)}), bf16[48,24,256]{2,1,0:T(8,128)(2,1)S(1)}, u32[]{:S(2)}, u32[]{:S(2)}) async-start(bf16[48,24,256]{2,1,0:T(8,128)(2,1)} %bitcast.27), calls=%async_computation | async-start | bytes 1179648 | tf_op jit(solution)/shard_map/all_to_all | solution.py:389
  24.3 4.0 %copy-start.7 = (f32[4096]{0:T(1024)S(1)}, f32[4096]{0:T(1024)}, u32[]{:S(2)}) copy-start(f32[4096]{0:T(1024)} %param.8) | copy-start | bytes 49156
  24.3 9.1 %copy-start.8 = (s32[1024]{0:T(1024)S(1)}, s32[1024]{0:T(1024)}, u32[]{:S(2)}) copy-start(s32[1024]{0:T(1024)} %param.9) | copy-start | bytes 12292
  48.8 12.2 %copy-start.4 = (s32[1,48,20]{1,0,2:T(1,128)S(1)}, s32[1,48,20]{1,0,2:T(1,128)}, u32[]{:S(2)}) copy-start(s32[1,48,20]{1,0,2:T(1,128)} %param.11) | copy-start | bytes 11524
  48.8 12.2 %copy-start.5 = (s32[1,48]{1,0:T(1,128)S(1)}, s32[1,48]{1,0:T(1,128)}, u32[]{:S(2)}) copy-start(s32[1,48]{1,0:T(1,128)} %counts_ref.3) | copy-start | bytes 580
  50.4 27.9 %all-to-all-start.1 = ((bf16[16,64,256]{2,1,0:T(8,128)(2,1)}), bf16[16,64,256]{2,1,0:T(8,128)(2,1)S(1)}, u32[]{:S(2)}, u32[]{:S(2)}) async-start(bf16[16,64,256]{2,1,0:T(8,128)(2,1)} %bitcast.28), calls=%async_computation.1 | async-start | bytes 1048576 | tf_op jit(solution)/shard_map/all_to_all | solution.py:416
  62.0 0.8 copy-start.2
  63.6 0.8 copy-start.1
  64.4 35.6 %copy-start = (bf16[4096,256]{1,0:T(8,128)(2,1)S(1)}, bf16[4096,256]{1,0:T(8,128)(2,1)}, u32[]{:S(2)}) copy-start(bf16[4096,256]{1,0:T(8,128)(2,1)} %broadcast_select_fusion.table_ref) | copy-start | bytes 6291460
  78.6 29.4 %copy-start.3 = (bf16[1920,128]{1,0:T(8,128)(2,1)S(1)}, bf16[1920,128]{1,0:T(8,128)(2,1)}, u32[]{:S(2)}) copy-start(bf16[1920,128]{1,0:T(8,128)(2,1)} %copy-done.2) | copy-start | bytes 1474564
  78.6 29.3 %all-to-all-start.2 = ((bf16[48,40,128]{2,1,0:T(8,128)(2,1)}), bf16[48,40,128]{2,1,0:T(8,128)(2,1)S(1)}, u32[]{:S(2)}, u32[]{:S(2)}) async-start(bf16[48,40,128]{2,1,0:T(8,128)(2,1)} %copy-done.1), calls=%async_computation.2 | async-start | bytes 983040 | tf_op jit(solution)/shard_map/all_to_all | solution.py:424

commit v3 on v2

--- a/solution.py
+++ b/solution.py
@@ -201,22 +201,30 @@
     return got
 
 
-def hits_kernel(capacity, got_ref, column_ref, hits_ref):
-    hit_matrix(got_ref, column_ref, hits_ref, capacity)
-
-
-def find_hits(got, column, capacity):
+def hits_kernel(capacity, got_ref, column_ref, theirs_ref, ours_ref, hits):
+    got = hit_matrix(got_ref, column_ref, hits, capacity)
+    half = theirs_ref.shape[0]
+    theirs_ref[...] = dot(hits[0:half, :], got).astype(bf16)
+    ours_ref[...] = dot(hits[half:, :], got)
+
+
+def partial_sums(got, column, capacity):
     flat, width = got.shape
     touch = column.shape[0]
     return pl.pallas_call(
         functools.partial(hits_kernel, capacity),
-        out_shape=jax.ShapeDtypeStruct((touch, flat), bf16),
+        out_shape=(
+            jax.ShapeDtypeStruct((touch // 2, width), bf16),
+            jax.ShapeDtypeStruct((touch // 2, width), f32),
+        ),
+        scratch_shapes=[pltpu.VMEM((touch, flat), bf16)],
         compiler_params=params,
         name="hits",
     )(got, column)
 
 
-def pick_kernel(hits, values_ref, out_ref):
+def pick_kernel(capacity, got_ref, column_ref, values_ref, out_ref, hits):
+    hit_matrix(got_ref, column_ref, hits, capacity)
     shards, pack, half = out_ref.shape
     whole = 16
     rest = pack // 2 - whole
@@ -231,39 +239,46 @@
     ).astype(bf16)
 
 
-def pick_rows(hits, values, shards, capacity):
-    return pl.pallas_call(
-        pick_kernel,
+def pick_rows(got, column, values, shards, capacity):
+    return pl.pallas_call(
+        functools.partial(pick_kernel, capacity),
         out_shape=jax.ShapeDtypeStruct((shards, 2 * capacity, values.shape[1] // 2), bf16),
+        scratch_shapes=[pltpu.VMEM((values.shape[0], got.shape[0]), bf16)],
         compiler_params=params,
         name="pick",
-    )(hits, values)
+    )(got, column, values)
 
 
 def update_kernel(offset_ref, parts_ref, previous_ref, state_ref, out_ref):
-    replicas, mine, width = parts_ref.shape
-    grad = parts_ref[0].astype(f32)
-    for k in range(1, replicas):
-        grad = grad + parts_ref[k].astype(f32)
-    grad = grad / replicas
+    replicas, chunk, width = parts_ref.shape
+    mine = 2 * chunk
+    halves = []
+    for core in range(2):
+        total = parts_ref[core].astype(f32)
+        for k in range(core + 2, replicas, 2):
+            total = total + parts_ref[k].astype(f32)
+        halves.append(total)
+    grad = jnp.concatenate(halves, axis=0) / replicas
     state = state_ref[...] + jnp.mean(grad * grad, axis=1, keepdims=True)
     out_ref[0:mine, :] = (
         previous_ref[...].astype(f32) - learn_rate * grad / (jnp.sqrt(state) + epsilon)
     ).astype(bf16)
-    shape = (mine, width)
-    at = iota(shape, 1) == iota(shape, 0) + offset_ref[0]
-    line = jnp.sum(jnp.where(at, state, 0.0), axis=0, keepdims=True)
-    first = line.astype(bf16).astype(f32)
-    second = (line - first).astype(bf16).astype(f32)
-    third = line - first - second
+    at = iota((chunk, width), 1) == iota((chunk, width), 0) + offset_ref[0]
     sub = iota((16, width), 0)
-    out_ref[mine : mine + 16, :] = jnp.where(
-        sub == 0, first, jnp.where(sub == 1, second, jnp.where(sub == 2, third, 0.0))
-    ).astype(bf16)
+    lines = jnp.zeros((16, width), f32)
+    for core in range(2):
+        own = state[core * chunk : (core + 1) * chunk]
+        line = jnp.sum(jnp.where(at, own, 0.0), axis=0, keepdims=True)
+        first = line.astype(bf16).astype(f32)
+        second = (line - first).astype(bf16).astype(f32)
+        for k, piece in enumerate((first, second, line - first - second)):
+            lines = jnp.where(sub == 3 * core + k, piece, lines)
+    out_ref[mine : mine + 16, :] = lines.astype(bf16)
 
 
 def update_rows(offset, parts, previous, state):
-    _, mine, width = parts.shape
+    _, chunk, width = parts.shape
+    mine = 2 * chunk
     vmem = pl.BlockSpec(memory_space=pltpu.VMEM)
     return pl.pallas_call(
         update_kernel,
@@ -286,16 +301,22 @@
     @pl.when(step == 0)
     def _():
         values[touch:, :] = jnp.zeros((256, width), bf16)
+        chunk = mine // 2
         for k in range(replicas):
-            values[k * mine : (k + 1) * mine, :] = every_ref[k * stride : k * stride + mine, :]
-        group = width // mine
+            for core in range(2):
+                at = core * (touch // 2) + k * chunk
+                source = k * stride + core * chunk
+                values[at : at + chunk, :] = every_ref[source : source + chunk, :]
+        group = width // chunk
         pieces = []
         for q in range(replicas // group):
             lines = jnp.zeros((16, width), f32)
             for k in range(q * group, (q + 1) * group):
                 lines = lines + every_ref[k * stride + mine : (k + 1) * stride, :].astype(f32)
             pieces.append(lines)
-        lines = jnp.concatenate(pieces, axis=1)
+        lines = jnp.concatenate(
+            [lines[3 * core : 3 * core + 3] for core in range(2) for lines in pieces], axis=1
+        )
         high = state_ref.shape[0]
         listed = listed_ref[...]
         at_high = iota((high, touch), 0) == (listed >> 7)
@@ -391,37 +412,45 @@
     ).reshape(shards * block, width)
 
     listed = sort_list(touched_rows)
-    column = jnp.broadcast_to(listed.reshape(touch, 1).astype(f32), (touch, 128))
+    replica = lax.axis_index("replica")
+    half = touch // 2
     order = listed.reshape(touch)
+    core = lax.rem(replica, 2)
+    theirs = lax.dynamic_slice(order, ((1 - core) * half,), (half,))
+    ours = lax.dynamic_slice(order, (core * half,), (half,))
+    turned = jnp.concatenate([theirs, ours])
+    column = jnp.broadcast_to(turned.reshape(touch, 1).astype(f32), (touch, 128))
     bounds = jnp.arange(rows // 128, dtype=jnp.int32) * 128
     starts = jnp.sum((touched_rows[None, :] < bounds[:, None]).astype(jnp.int32), axis=1)
-    replica = lax.axis_index("replica")
-    values = jnp.take(table, order, axis=0, mode="clip")
-    mine_values = lax.dynamic_slice(values, (replica * mine, 0), (mine, width))
-    mine_rows = lax.dynamic_slice(order, (replica * mine,), (mine,))
+    values = jnp.take(table, turned, axis=0, mode="clip")
+    chunk = mine // 2
+    mine_rows = lax.dynamic_slice(order.reshape(2, half), (0, replica * chunk), (2, chunk))
+    mine_rows = mine_rows.reshape(mine)
+    mine_values = jnp.take(table, mine_rows, axis=0, mode="clip")
     mine_state = jnp.take(row_state, mine_rows, mode="clip")[:, None]
     marked = jnp.zeros(row_state.shape, f32).at[touched_rows].set(
         1.0, mode="promise_in_bounds", unique_indices=True
     )
     kept_state = jnp.where(marked > 0, 0.0, row_state)
     kept_table = jnp.where(marked[:, None] > 0, jnp.zeros((), bf16), table)
-    got, column, kept_state, kept_table, mine_state, mine_values, starts = (
+    got, column, values, kept_state, kept_table, mine_state, mine_values, starts = (
         lax.optimization_barrier(
-            (got, column, kept_state, kept_table, mine_state, mine_values, starts)
+            (got, column, values, kept_state, kept_table, mine_state, mine_values, starts)
         )
     )
 
-    hits = find_hits(got, column, capacity)
-    part = dot(hits, got).astype(bf16)
+    theirs, ours = partial_sums(got, column, capacity)
+    theirs = lax.ppermute(theirs, "replica", [(k, k ^ 1) for k in range(replicas)])
+    part = (ours + theirs.astype(f32)).astype(bf16)
     parts = lax.all_to_all(
-        part.reshape(replicas, mine, width), "replica", split_axis=0, concat_axis=0, tiled=True
-    )
-    picked = pick_rows(hits, values, shards, capacity)
+        part.reshape(replicas, chunk, width), "replica", split_axis=0, concat_axis=0, tiled=True
+    )
+    picked = pick_rows(got, column, values, shards, capacity)
     member = member_matrix(bags, route_counts)
-    offset = (lax.rem(replica, width // mine) * mine).astype(jnp.int32).reshape(1)
+    offset = (lax.rem(replica, width // chunk) * chunk).astype(jnp.int32).reshape(1)
+    picked, member, parts = lax.optimization_barrier((picked, member, parts))
+    returned = lax.all_to_all(picked, "shard", split_axis=0, concat_axis=0, tiled=True)
     updated = update_rows(offset, parts, mine_values, mine_state)
-    picked, member, updated = lax.optimization_barrier((picked, member, updated))
-    returned = lax.all_to_all(picked, "shard", split_axis=0, concat_axis=0, tiled=True)
     every = lax.all_gather(updated, "replica", axis=0, tiled=True)
     new_table, new_state = place_rows(starts, every, listed, kept_table, kept_state, mine, tile)
     pooled = pool_rows(member, returned, bag_count)

time: 109 us -> 105 us (0.963)
  waiting for transfers between devices: 30.9 us -> 20.5 us
  local copies, waits for them, and re-layouts: 11.2 us -> 14.6 us
  starting transfers between devices: 34.5 us -> 36.6 us
  other arithmetic: 2.66 us -> 4.34 us
  matrix products: 1.64 us -> 0 us
    all_to_all x1, waiting for transfers between devices: 13.9 us -> 6.99 us  [local(): lax.all_to_all(part.reshape(replicas, chunk, width), 'replica', split_axi...]
    ppermute x0 -> x1, starting transfers between devices: none -> 5.35 us  [local(): lax.ppermute(theirs, 'replica', [(k, k ^ 1) for k in range(replicas)])]
    all_to_all x1, waiting for transfers between devices: 12.5 us -> 9.19 us  [local(): lax.all_to_all(send.reshape(shards, block, width), 'shard', split_axis=0,...]
    all_to_all x1, starting transfers between devices: 10.6 us -> 7.48 us  [local(): lax.all_to_all(part.reshape(replicas, chunk, width), 'replica', split_axi...]
    gather x1 -> x2, local copies, waits for them, and re-layouts: 3.94 us -> 5.66 us  [the longest x1 4.96 us: local(): values = jnp.take(table, turned, axis=0, mode='clip')]
    dot_general x1 -> x0, matrix products: 1.64 us -> none  [dot(): return jnp.dot(a, b, preferred_element_type=f32)]
    all_to_all x1, waiting for transfers between devices: 4.56 us -> 3.17 us  [local(): lax.all_to_all(picked, 'shard', split_axis=0, concat_axis=0, tiled=True)]
    ppermute x0 -> x1, waiting for transfers between devices: none -> 1.14 us  [local(): lax.ppermute(theirs, 'replica', [(k, k ^ 1) for k in range(replicas)])]
  transfers between devices with their start and end apart: 3 -> 4, of which waited for: 3 -> 4; matrix products, arithmetic and copies ran while one was open for 11% -> 15% of each run, Pallas kernels for 6% -> 6%
where the time goes in v3:
time: 105 us
  starting transfers between devices  36.6 us (35%)
  waiting for transfers between devices  20.5 us (20%)
  blocking collectives  16.3 us (16%)
  local copies, waits for them, and re-layouts  14.6 us (14%)
  Pallas kernels  11.5 us (11%)
  other arithmetic  4.34 us (4%)
    all_to_all x1, starting transfers between devices, local(): lax.all_to_all(send.reshape(shards, block, width), 'shard', split_axis=0,...  18.9 us
    all_gather x1, blocking collectives, local(): every = lax.all_gather(updated, 'replica', axis=0, tiled=True)  16.3 us
    all_to_all x1, waiting for transfers between devices, local(): lax.all_to_all(send.reshape(shards, block, width), 'shard', split_axis=0,...  9.19 us
    all_to_all x1, starting transfers between devices, local(): lax.all_to_all(part.reshape(replicas, chunk, width), 'replica', split_axi...  7.48 us
    all_to_all x1, waiting for transfers between devices, local(): lax.all_to_all(part.reshape(replicas, chunk, width), 'replica', split_axi...  6.99 us
    ppermute x1, starting transfers between devices, local(): lax.ppermute(theirs, 'replica', [(k, k ^ 1) for k in range(replicas)])  5.35 us
    gather x1, local copies, waits for them, and re-layouts, local(): values = jnp.take(table, turned, axis=0, mode='clip')  4.96 us
    all_to_all x1, starting transfers between devices, local(): lax.all_to_all(picked, 'shard', split_axis=0, concat_axis=0, tiled=True)  4.94 us
  transfers between devices with their start and end apart: 4, of which 4 were waited for; matrix products, arithmetic and copies ran while one was open for 15% of the time, Pallas kernels for 6%

profile of v3, /device:TPU:1, one launch (start us, length us, event | category | flops | bytes accessed | tf_op | source)
XLA Modules:
  0.0 104.7 jit_solution(18398151186012943718)
XLA Ops:
  0.6 2.6 %prep.1 = bf16[1152,256]{1,0:T(8,128)(2,1)} custom-call(s32[20,1,48]{2,1,0:T(1,128)} %bitcast.24, s32[20,1,48]{2,1,0:T(1,128)} %bitcast.18, s32[1,48]{1,0:T(1,128)} %counts_ref.3, f32[40,256]{1,0:T(8,128)} %grad_ref.1), custom_call_target="tpu_custom_call" | custom-call | tf_op jit(solution)/shard_map/prep/pallas_call | solution.py:97
  3.3 18.9 %all-to-all-start = ((bf16[48,24,256]{2,1,0:T(8,128)(2,1)}), bf16[48,24,256]{2,1,0:T(8,128)(2,1)S(1)}, u32[]{:S(2)}, u32[]{:S(2)}) async-start(bf16[48,24,256]{2,1,0:T(8,128)(2,1)} %bitcast.22), calls=%async_computation | async-start | bytes 1179648 | tf_op jit(solution)/shard_map/all_to_all | solution.py:410
  22.2 0.8 compare_select_fusion
  23.2 1.0 sort.1.listed_ref
  25.6 5.0 %gather_fusion = bf16[1024,256]{1,0:T(8,128)(2,1)} fusion(bf16[4096,256]{1,0:T(8,128)(2,1)S(1)} %copy-done.6, s32[1024]{0:T(1024)S(1)} %get-tuple-element.37), kind=kCustom, calls=%fused_computation | custom fusion | bytes 1052672 | tf_op jit(solution)/shard_map/jit(_take)/gather | solution.py:425
  31.3 0.8 gather_fusion.1
  32.1 4.3 %scatter_custom_fusion = f32[4096]{0:T(1024)S(1)} fusion(s32[1024]{0:T(1024)S(1)} %get-tuple-element.35, f32[1024]{0:T(1024)S(1)} %broadcast.15, f32[]{:T(128)} %constant.9.clone.1), kind=kCustom, calls=%fused_computation.10 | custom fusion | bytes 16388 | tf_op jit(solution)/shard_map/scatter | solution.py:431
  36.6 1.9 %broadcast_select_fusion.table_ref = bf16[4096,256]{1,0:T(8,128)(2,1)S(1)} fusion(bf16[4096,256]{1,0:T(8,128)(2,1)} %param.7, pred[4096]{0:T(1024)(128)(4,1)S(1)} %get-tuple-element.34), kind=kLoop, calls=%fused_computation.4 | loop fusion | flops 1048576 | bytes 4198400 | tf_op jit(solution)/shard_map/jit(_where)/select_n | solution.py:435
  38.6 9.2 %all-to-all-done = bf16[48,24,256]{2,1,0:T(8,128)(2,1)S(1)} async-done(((bf16[48,24,256]{2,1,0:T(8,128)(2,1)}), bf16[48,24,256]{2,1,0:T(8,128)(2,1)S(1)}, u32[]{:S(2)}, u32[]{:S(2)}) %all-to-all-start) | async-done | bytes 589856 | tf_op jit(solution)/shard_map/all_to_all | solution.py:410
  48.0 1.1 %hits.1 = (bf16[512,256]{1,0:T(8,128)(2,1)S(1)}, f32[512,256]{1,0:T(8,128)S(1)}) custom-call(bf16[1152,256]{1,0:T(8,128)(2,1)S(1)} %bitcast.14, f32[1024,128]{1,0:T(8,128)S(1)} %broadcast_in_dim.39.column_ref), custom_call_target="tpu_custom_call" | custom-call | tf_op jit(solution)/shard_map/hits/pallas_call | solution.py:214
  49.1 5.4 %collective-permute-start = (bf16[512,256]{1,0:T(8,128)(2,1)S(1)}, bf16[512,256]{1,0:T(8,128)(2,1)S(1)}, u32[]{:S(2)}, u32[]{:S(2)}) collective-permute-start(bf16[512,256]{1,0:T(8,128)(2,1)S(1)} %get-tuple-element.22), channel_id=1, source_target_pairs={{0,48},{48,0},{96,144},{144,96},{192,240},{240,192},{288,336},{336... | collective-permute-start | bytes 786440 | tf_op jit(solution)/shard_map/ppermute | solution.py:443
  54.5 1.1 %collective-permute-done = bf16[512,256]{1,0:T(8,128)(2,1)S(1)} collective-permute-done((bf16[512,256]{1,0:T(8,128)(2,1)S(1)}, bf16[512,256]{1,0:T(8,128)(2,1)S(1)}, u32[]{:S(2)}, u32[]{:S(2)}) %collective-permute-start) | collective-permute-done | bytes 262176 | tf_op jit(solution)/shard_map/ppermute | solution.py:443
  56.4 7.5 %all-to-all-start.1 = ((bf16[16,32,256]{2,1,0:T(8,128)(2,1)}), bf16[16,32,256]{2,1,0:T(8,128)(2,1)S(1)}, u32[]{:S(2)}, u32[]{:S(2)}) async-start(bf16[16,32,256]{2,1,0:T(8,128)(2,1)} %bitcast.23), calls=%async_computation.1 | async-start | bytes 524288 | tf_op jit(solution)/shard_map/all_to_all | solution.py:445
  63.9 0.9 member.1.member_ref
  64.8 0.8 copy-done.1
  65.6 1.0 copy-done
  66.6 1.1 %pick.1 = bf16[48,40,128]{2,1,0:T(8,128)(2,1)S(1)} custom-call(bf16[1152,256]{1,0:T(8,128)(2,1)S(1)} %bitcast.15, f32[1024,128]{1,0:T(8,128)S(1)} %broadcast_in_dim.39.column_ref, bf16[1024,256]{1,0:T(8,128)(2,1)S(1)} %copy-done), custom_call_target="tpu_custom_call" | custom-call | tf_op jit(solution)/shard_map/pick/pallas_call | solution.py:243
  67.8 0.8 copy-done.3
  68.6 7.0 %all-to-all-done.1.parts_ref = bf16[16,32,256]{2,1,0:T(8,128)(2,1)S(1)} async-done(((bf16[16,32,256]{2,1,0:T(8,128)(2,1)}), bf16[16,32,256]{2,1,0:T(8,128)(2,1)S(1)}, u32[]{:S(2)}, u32[]{:S(2)}) %all-to-all-start.1) | async-done | bytes 262176 | tf_op jit(solution)/shard_map/all_to_all | solution.py:445
  75.6 4.9 %all-to-all-start.2 = ((bf16[48,40,128]{2,1,0:T(8,128)(2,1)}), bf16[48,40,128]{2,1,0:T(8,128)(2,1)S(1)}, u32[]{:S(2)}, u32[]{:S(2)}) async-start(bf16[48,40,128]{2,1,0:T(8,128)(2,1)} %copy-done.3), calls=%async_computation.2 | async-start | bytes 983040 | tf_op jit(solution)/shard_map/all_to_all | solution.py:452
  80.9 16.3 %all_gather.3.every_ref = bf16[1280,256]{1,0:T(8,128)(2,1)S(1)} all-gather(bf16[80,256]{1,0:T(8,128)(2,1)S(1)} %update.1), channel_id=1, replica_groups=mesh['replica'=16,'shard'=48] {'replica'}, dimensions={0}, use_global_device_ids=true | all-gather | bytes 696320 | tf_op jit(solution)/shard_map/all_gather | solution.py:454
  97.1 3.4 %place.1 = (bf16[4096,256]{1,0:T(8,128)(2,1)}, f32[32,128]{1,0:T(8,128)}) custom-call(s32[32]{0:T(128)S(1)} %convert_reduce_fusion.starts, bf16[1280,256]{1,0:T(8,128)(2,1)S(1)} %all_gather.3.every_ref, s32[1,1024]{1,0:T(1,128)S(1)} %sort.1.listed_ref, s32[16,128]{1,0:T(8,128)S(1)} %pad.4.tiles_ref, bf16[4096,256]{1,0:T(8,128)(2,1)S(1)} %broadcast_select_fusion.table_ref, ...), custom_call_target="tpu_custom_call" | custom-call | tf_op jit(solution)/shard_map/place/pallas_call | solution.py:354
  100.5 3.2 %all-to-all-done.2.rows_ref = bf16[48,40,128]{2,1,0:T(8,128)(2,1)S(1)} async-done(((bf16[48,40,128]{2,1,0:T(8,128)(2,1)}), bf16[48,40,128]{2,1,0:T(8,128)(2,1)S(1)}, u32[]{:S(2)}, u32[]{:S(2)}) %all-to-all-start.2) | async-done | bytes 491552 | tf_op jit(solution)/shard_map/all_to_all | solution.py:452
  103.7 1.0 pool.1
  (34 shorter events, 3.8 us)
Async XLA Ops:
  0.6 25.0 %copy-start.6 = (bf16[4096,256]{1,0:T(8,128)(2,1)S(1)}, bf16[4096,256]{1,0:T(8,128)(2,1)}, u32[]{:S(2)}) copy-start(bf16[4096,256]{1,0:T(8,128)(2,1)} %param.7) | copy-start | bytes 6291460
  3.3 44.5 %all-to-all-start = ((bf16[48,24,256]{2,1,0:T(8,128)(2,1)}), bf16[48,24,256]{2,1,0:T(8,128)(2,1)S(1)}, u32[]{:S(2)}, u32[]{:S(2)}) async-start(bf16[48,24,256]{2,1,0:T(8,128)(2,1)} %bitcast.22), calls=%async_computation | async-start | bytes 1179648 | tf_op jit(solution)/shard_map/all_to_all | solution.py:410
  25.6 5.7 %copy-start.7 = (f32[4096]{0:T(1024)S(1)}, f32[4096]{0:T(1024)}, u32[]{:S(2)}) copy-start(f32[4096]{0:T(1024)} %param.8) | copy-start | bytes 49156
  25.6 10.8 %copy-start.8 = (s32[1024]{0:T(1024)S(1)}, s32[1024]{0:T(1024)}, u32[]{:S(2)}) copy-start(s32[1024]{0:T(1024)} %param.9) | copy-start | bytes 12292
  38.6 25.3 %copy-start.4 = (s32[1,48,20]{1,0,2:T(1,128)S(1)}, s32[1,48,20]{1,0,2:T(1,128)}, u32[]{:S(2)}) copy-start(s32[1,48,20]{1,0,2:T(1,128)} %param.11) | copy-start | bytes 11524
  38.6 25.3 %copy-start.5 = (s32[1,48]{1,0:T(1,128)S(1)}, s32[1,48]{1,0:T(1,128)}, u32[]{:S(2)}) copy-start(s32[1,48]{1,0:T(1,128)} %counts_ref.3) | copy-start | bytes 580
  49.1 6.5 %collective-permute-start = (bf16[512,256]{1,0:T(8,128)(2,1)S(1)}, bf16[512,256]{1,0:T(8,128)(2,1)S(1)}, u32[]{:S(2)}, u32[]{:S(2)}) collective-permute-start(bf16[512,256]{1,0:T(8,128)(2,1)S(1)} %get-tuple-element.22), channel_id=1, source_target_pairs={{0,48},{48,0},{96,144},{144,96},{192,240},{240,192},{288,336},{336... | collective-permute-start | bytes 786440 | tf_op jit(solution)/shard_map/ppermute | solution.py:443
  56.4 19.2 %all-to-all-start.1 = ((bf16[16,32,256]{2,1,0:T(8,128)(2,1)}), bf16[16,32,256]{2,1,0:T(8,128)(2,1)S(1)}, u32[]{:S(2)}, u32[]{:S(2)}) async-start(bf16[16,32,256]{2,1,0:T(8,128)(2,1)} %bitcast.23), calls=%async_computation.1 | async-start | bytes 524288 | tf_op jit(solution)/shard_map/all_to_all | solution.py:445
  64.8 0.8 copy-start.1
  65.6 1.0 copy-start
  67.8 0.8 copy-start.3
  75.6 28.2 %all-to-all-start.2 = ((bf16[48,40,128]{2,1,0:T(8,128)(2,1)}), bf16[48,40,128]{2,1,0:T(8,128)(2,1)S(1)}, u32[]{:S(2)}, u32[]{:S(2)}) async-start(bf16[48,40,128]{2,1,0:T(8,128)(2,1)} %copy-done.3), calls=%async_computation.2 | async-start | bytes 983040 | tf_op jit(solution)/shard_map/all_to_all | solution.py:452
  80.5 23.2 %copy-start.2 = (bf16[1920,128]{1,0:T(8,128)(2,1)S(1)}, bf16[1920,128]{1,0:T(8,128)(2,1)}, u32[]{:S(2)}) copy-start(bf16[1920,128]{1,0:T(8,128)(2,1)} %copy-done.1) | copy-start | bytes 1474564

commit v4 on v3

--- a/solution.py
+++ b/solution.py
@@ -30,16 +30,6 @@
     return (position * 2731) >> 16
 
 
-def slot_of(shape):
-    position = iota(shape, 0)
-    return position - block * pair_of(position)
-
-
-def spread_matrix(shards):
-    shape = (shards * block, shards)
-    return jnp.where(pair_of(iota(shape, 0)) == iota(shape, 1), 1.0, 0.0)
-
-
 def keys_of(bags_ref, counts_ref):
     capacity, _, shards = bags_ref.shape
     bags = bags_ref[...].reshape(capacity, shards)
@@ -60,12 +50,15 @@
     bag_count, width = grad_ref.shape
     flat = shards * block
     key = keys_of(bags_ref, counts_ref)
-    spread = spread_matrix(shards)
-    per_row = dot_nt(spread.astype(bf16), key)
-    own = slot_of((flat, capacity)) == iota((flat, capacity), 1)
-    bag = dot(jnp.where(own, per_row, 0.0).astype(bf16), jnp.ones((capacity, 128), bf16))
-    match = (bag == iota((flat, 128), 1).astype(f32)) & (slot_of((flat, 128)) < capacity)
-    member = jnp.where(match, 1.0, 0.0).astype(bf16)
+    position, lane = iota((flat, 128), 0), iota((flat, 128), 1)
+    pair = pair_of(position)
+    slot = position - block * pair
+    spread = jnp.where(pair == lane, 1.0, 0.0)
+    per_row = dot_nt(spread.astype(bf16)[:, 0:shards], key)
+    per_row = jnp.where((slot == lane)[:, 0:capacity], per_row, 0.0).astype(bf16)
+    bag = dot(per_row, jnp.ones((capacity, 128), bf16))
+    bag = jnp.where(slot < capacity, bag, float(dead))
+    member = jnp.where(bag == lane.astype(f32), 1.0, 0.0).astype(bf16)
     grads = jnp.concatenate(
         [grad_ref[...], jnp.zeros((128 - bag_count, width), f32)], axis=0
     ).astype(bf16)
@@ -77,7 +70,7 @@
     meta = dot(jnp.where(lane == sub, 1.0, 0.0).astype(bf16), high) + dot(
         jnp.where(lane == sub + 128, 1.0, 0.0).astype(bf16), low
     )
-    at_meta = jnp.where(slot_of((flat, shards)) == capacity, spread, 0.0).astype(bf16)
+    at_meta = jnp.where(slot == capacity, spread, 0.0).astype(bf16)[:, 0:shards]
     meta = meta.astype(bf16)
     pieces = sems.shape[0]
     size = flat // pieces
@@ -126,29 +119,29 @@
     flat = shards * pack
     key = keys_of(bags_ref, counts_ref)
 
-    def pair_and_place(shape):
-        row = iota(shape, 0)
+    def pair_and_place(shape, axis):
+        row = iota(shape, axis)
         pair = (row * 13108) >> 19
         return pair, row - pack * pair
 
-    shape = (flat, shards)
-    spread = jnp.where(pair_and_place(shape)[0] == iota(shape, 1), 1.0, 0.0).astype(bf16)
-    per_row = dot_nt(spread, key)
-    shape = (flat, capacity)
-    slot, _ = packed_slot(pair_and_place(shape)[1], capacity)
-    own = jnp.where(slot == iota(shape, 1), per_row, 0.0).astype(bf16)
-    bag = dot(own, jnp.ones((capacity, 128), bf16))
-    shape = (flat, 128)
-    _, right = packed_slot(pair_and_place(shape)[1], capacity)
+    shape = (shards, flat)
+    spread = jnp.where(pair_and_place(shape, 1)[0] == iota(shape, 0), 1.0, 0.0).astype(bf16)
+    per_row = dot(key, spread)
+    shape = (capacity, flat)
+    slot, _ = packed_slot(pair_and_place(shape, 1)[1], capacity)
+    own = jnp.where(slot == iota(shape, 0), per_row, 0.0).astype(bf16)
+    bag = dot(jnp.ones((128, capacity), bf16), own)
+    shape = (128, flat)
+    _, right = packed_slot(pair_and_place(shape, 1)[1], capacity)
     bag = bag + jnp.where(right, 64.0, 0.0)
-    out_ref[...] = jnp.where(bag == iota(shape, 1).astype(f32), 1.0, 0.0).astype(bf16)
+    out_ref[...] = jnp.where(bag == iota(shape, 0).astype(f32), 1.0, 0.0).astype(bf16)
 
 
 def member_matrix(bags, counts):
     capacity, _, shards = bags.shape
     return pl.pallas_call(
         member_kernel,
-        out_shape=jax.ShapeDtypeStruct((shards * 2 * capacity, 128), bf16),
+        out_shape=jax.ShapeDtypeStruct((128, shards * 2 * capacity), bf16),
         compiler_params=params,
         name="member",
     )(bags, counts)
@@ -379,17 +372,15 @@
 
 
 def pool_kernel(member_ref, rows_ref, out_ref):
-    shards, pack, half = rows_ref.shape
     bag_count = out_ref.shape[0]
-    rows = rows_ref[...].astype(f32).reshape(shards * pack, half).astype(bf16)
-    total = dot_tn(member_ref[...], rows)
+    total = dot(member_ref[...], rows_ref[...])
     out_ref[...] = jnp.concatenate([total[0:bag_count], total[64 : 64 + bag_count]], axis=1)
 
 
 def pool_rows(member, rows, bag_count):
     return pl.pallas_call(
         pool_kernel,
-        out_shape=jax.ShapeDtypeStruct((bag_count, 2 * rows.shape[2]), f32),
+        out_shape=jax.ShapeDtypeStruct((bag_count, 2 * rows.shape[1]), f32),
         compiler_params=params,
         name="pool",
     )(member, rows)
@@ -440,7 +431,9 @@
     )
 
     theirs, ours = partial_sums(got, column, capacity)
-    theirs = lax.ppermute(theirs, "replica", [(k, k ^ 1) for k in range(replicas)])
+    pairs = [[k, k + 1] for k in range(0, replicas, 2)]
+    both = lax.all_gather(theirs, "replica", axis=0, tiled=True, axis_index_groups=pairs)
+    theirs = lax.dynamic_slice(both, ((1 - core) * half, 0), (half, width))
     part = (ours + theirs.astype(f32)).astype(bf16)
     parts = lax.all_to_all(
         part.reshape(replicas, chunk, width), "replica", split_axis=0, concat_axis=0, tiled=True
@@ -453,7 +446,7 @@
     updated = update_rows(offset, parts, mine_values, mine_state)
     every = lax.all_gather(updated, "replica", axis=0, tiled=True)
     new_table, new_state = place_rows(starts, every, listed, kept_table, kept_state, mine, tile)
-    pooled = pool_rows(member, returned, bag_count)
+    pooled = pool_rows(member, returned.reshape(-1, width // 2), bag_count)
     return (pooled, new_table, new_state.reshape(row_state.shape))
 
 

time: 105 us -> 104 us (level)
  starting transfers between devices: 36.6 us -> 31.3 us
  blocking collectives: 16.3 us -> 21.5 us
    ppermute x1 -> x0, starting transfers between devices: 5.35 us -> none  [local(): lax.ppermute(theirs, 'replica', [(k, k ^ 1) for k in range(replicas)])]
    all_gather x0 -> x1, blocking collectives: none -> 5.18 us  [local(): lax.all_gather(theirs, 'replica', axis=0, tiled=True, axis_index_groups=p...]
    ppermute x1 -> x0, waiting for transfers between devices: 1.14 us -> none  [local(): lax.ppermute(theirs, 'replica', [(k, k ^ 1) for k in range(replicas)])]
  transfers between devices with their start and end apart: 4 -> 3, of which waited for: 4 -> 3; matrix products, arithmetic and copies ran while one was open for 15% -> 15% of each run, Pallas kernels for 6% -> 6%
where the time goes in v4:
time: 104 us; the launch traced here: 103 us
  starting transfers between devices  31.3 us (30%)
  blocking collectives  21.5 us (21%)
  waiting for transfers between devices  20 us (19%)
  local copies, waits for them, and re-layouts  14.6 us (14%)
  Pallas kernels  10.9 us (10%)
  other arithmetic  4.34 us (4%)
    all_to_all x1, starting transfers between devices, local(): lax.all_to_all(send.reshape(shards, block, width), 'shard', split_axis=0,...  18.8 us
    all_gather x1, blocking collectives, local(): every = lax.all_gather(updated, 'replica', axis=0, tiled=True)  16.3 us
    all_to_all x1, waiting for transfers between devices, local(): lax.all_to_all(send.reshape(shards, block, width), 'shard', split_axis=0,...  9.26 us
    all_to_all x1, waiting for transfers between devices, local(): lax.all_to_all(part.reshape(replicas, chunk, width), 'replica', split_axi...  7.55 us
    all_to_all x1, starting transfers between devices, local(): lax.all_to_all(part.reshape(replicas, chunk, width), 'replica', split_axi...  7.49 us
    all_gather x1, blocking collectives, local(): lax.all_gather(theirs, 'replica', axis=0, tiled=True, axis_index_groups=p...  5.18 us
    gather x1, local copies, waits for them, and re-layouts, local(): values = jnp.take(table, turned, axis=0, mode='clip')  4.96 us
    all_to_all x1, starting transfers between devices, local(): lax.all_to_all(picked, 'shard', split_axis=0, concat_axis=0, tiled=True)  4.94 us
  transfers between devices with their start and end apart: 3, of which 3 were waited for; matrix products, arithmetic and copies ran while one was open for 15% of the time, Pallas kernels for 6%

profile of v4, /device:TPU:1, one launch (start us, length us, event | category | flops | bytes accessed | tf_op | source)
XLA Modules:
  0.0 103.4 jit_solution(17404601990393374083)
XLA Ops:
  0.6 2.7 %prep.1 = bf16[1152,256]{1,0:T(8,128)(2,1)} custom-call(s32[20,1,48]{2,1,0:T(1,128)} %bitcast.26, s32[20,1,48]{2,1,0:T(1,128)} %bitcast.20, s32[1,48]{1,0:T(1,128)} %counts_ref.3, f32[40,256]{1,0:T(8,128)} %grad_ref.1), custom_call_target="tpu_custom_call" | custom-call | tf_op jit(solution)/shard_map/prep/pallas_call | solution.py:90
  3.3 18.8 %all-to-all-start = ((bf16[48,24,256]{2,1,0:T(8,128)(2,1)}), bf16[48,24,256]{2,1,0:T(8,128)(2,1)S(1)}, u32[]{:S(2)}, u32[]{:S(2)}) async-start(bf16[48,24,256]{2,1,0:T(8,128)(2,1)} %bitcast.24), calls=%async_computation | async-start | bytes 1179648 | tf_op jit(solution)/shard_map/all_to_all | solution.py:401
  22.2 0.8 compare_select_fusion
  23.2 1.0 sort.1.listed_ref
  25.6 5.0 %gather_fusion = bf16[1024,256]{1,0:T(8,128)(2,1)} fusion(bf16[4096,256]{1,0:T(8,128)(2,1)S(1)} %copy-done.6, s32[1024]{0:T(1024)S(1)} %get-tuple-element.37), kind=kCustom, calls=%fused_computation | custom fusion | bytes 1052672 | tf_op jit(solution)/shard_map/jit(_take)/gather | solution.py:416
  30.6 0.7 gather_fusion.2
  31.3 0.8 gather_fusion.1
  32.1 4.3 %scatter_custom_fusion = f32[4096]{0:T(1024)S(1)} fusion(s32[1024]{0:T(1024)S(1)} %get-tuple-element.35, f32[1024]{0:T(1024)S(1)} %broadcast.15, f32[]{:T(128)} %constant.9.clone.1), kind=kCustom, calls=%fused_computation.10 | custom fusion | bytes 16388 | tf_op jit(solution)/shard_map/scatter | solution.py:422
  36.6 1.9 %broadcast_select_fusion.table_ref = bf16[4096,256]{1,0:T(8,128)(2,1)S(1)} fusion(bf16[4096,256]{1,0:T(8,128)(2,1)} %param.7, pred[4096]{0:T(1024)(128)(4,1)S(1)} %get-tuple-element.34), kind=kLoop, calls=%fused_computation.4 | loop fusion | flops 1048576 | bytes 4198400 | tf_op jit(solution)/shard_map/jit(_where)/select_n | solution.py:426
  38.6 9.3 %all-to-all-done = bf16[48,24,256]{2,1,0:T(8,128)(2,1)S(1)} async-done(((bf16[48,24,256]{2,1,0:T(8,128)(2,1)}), bf16[48,24,256]{2,1,0:T(8,128)(2,1)S(1)}, u32[]{:S(2)}, u32[]{:S(2)}) %all-to-all-start) | async-done | bytes 589856 | tf_op jit(solution)/shard_map/all_to_all | solution.py:401
  48.0 1.1 %hits.1 = (bf16[512,256]{1,0:T(8,128)(2,1)S(1)}, f32[512,256]{1,0:T(8,128)S(1)}) custom-call(bf16[1152,256]{1,0:T(8,128)(2,1)S(1)} %bitcast.15, f32[1024,128]{1,0:T(8,128)S(1)} %broadcast_in_dim.39.column_ref), custom_call_target="tpu_custom_call" | custom-call | tf_op jit(solution)/shard_map/hits/pallas_call | solution.py:207
  49.2 5.2 %all_gather.6 = bf16[1024,256]{1,0:T(8,128)(2,1)S(1)} all-gather(bf16[512,256]{1,0:T(8,128)(2,1)S(1)} %get-tuple-element.22), channel_id=1, replica_groups={{0,48},{96,144},{192,240},{288,336},{384,432},{480,528},{576,624},{672,..., dimensions={0}, use_global_device_ids=true | all-gather | bytes 786432 | tf_op jit(solution)/shard_map/all_gather | solution.py:435
  54.4 0.8 add_convert_fusion
  55.1 7.5 %all-to-all-start.1 = ((bf16[16,32,256]{2,1,0:T(8,128)(2,1)}), bf16[16,32,256]{2,1,0:T(8,128)(2,1)S(1)}, u32[]{:S(2)}, u32[]{:S(2)}) async-start(bf16[16,32,256]{2,1,0:T(8,128)(2,1)} %bitcast.25), calls=%async_computation.1 | async-start | bytes 524288 | tf_op jit(solution)/shard_map/all_to_all | solution.py:438
  63.1 0.8 copy-done.1
  63.8 1.0 %copy-done = bf16[1024,256]{1,0:T(8,128)(2,1)S(1)} copy-done((bf16[1024,256]{1,0:T(8,128)(2,1)S(1)}, bf16[1024,256]{1,0:T(8,128)(2,1)}, u32[]{:S(2)}) %copy-start) | copy-done | bytes 524312
  64.9 1.1 %pick.1 = bf16[48,40,128]{2,1,0:T(8,128)(2,1)S(1)} custom-call(bf16[1152,256]{1,0:T(8,128)(2,1)S(1)} %bitcast.16, f32[1024,128]{1,0:T(8,128)S(1)} %broadcast_in_dim.39.column_ref, bf16[1024,256]{1,0:T(8,128)(2,1)S(1)} %copy-done), custom_call_target="tpu_custom_call" | custom-call | tf_op jit(solution)/shard_map/pick/pallas_call | solution.py:236
  66.0 0.8 copy-done.3
  66.8 7.5 %all-to-all-done.1.parts_ref = bf16[16,32,256]{2,1,0:T(8,128)(2,1)S(1)} async-done(((bf16[16,32,256]{2,1,0:T(8,128)(2,1)}), bf16[16,32,256]{2,1,0:T(8,128)(2,1)S(1)}, u32[]{:S(2)}, u32[]{:S(2)}) %all-to-all-start.1) | async-done | bytes 262176 | tf_op jit(solution)/shard_map/all_to_all | solution.py:438
  74.3 4.9 %all-to-all-start.2 = ((bf16[48,40,128]{2,1,0:T(8,128)(2,1)}), bf16[48,40,128]{2,1,0:T(8,128)(2,1)S(1)}, u32[]{:S(2)}, u32[]{:S(2)}) async-start(bf16[48,40,128]{2,1,0:T(8,128)(2,1)} %copy-done.3), calls=%async_computation.2 | async-start | bytes 983040 | tf_op jit(solution)/shard_map/all_to_all | solution.py:445
  79.6 16.3 %all_gather.7.every_ref = bf16[1280,256]{1,0:T(8,128)(2,1)S(1)} all-gather(bf16[80,256]{1,0:T(8,128)(2,1)S(1)} %update.1), channel_id=1, replica_groups=mesh['replica'=16,'shard'=48] {'replica'}, dimensions={0}, use_global_device_ids=true | all-gather | bytes 696320 | tf_op jit(solution)/shard_map/all_gather | solution.py:447
  95.9 3.4 %place.1 = (bf16[4096,256]{1,0:T(8,128)(2,1)}, f32[32,128]{1,0:T(8,128)}) custom-call(s32[32]{0:T(128)S(1)} %convert_reduce_fusion.starts, bf16[1280,256]{1,0:T(8,128)(2,1)S(1)} %all_gather.7.every_ref, s32[1,1024]{1,0:T(1,128)S(1)} %sort.1.listed_ref, s32[16,128]{1,0:T(8,128)S(1)} %pad.4.tiles_ref, bf16[4096,256]{1,0:T(8,128)(2,1)S(1)} %broadcast_select_fusion.table_ref, ...), custom_call_target="tpu_custom_call" | custom-call | tf_op jit(solution)/shard_map/place/pallas_call | solution.py:347
  99.3 3.2 %all-to-all-done.2 = bf16[48,40,128]{2,1,0:T(8,128)(2,1)S(1)} async-done(((bf16[48,40,128]{2,1,0:T(8,128)(2,1)}), bf16[48,40,128]{2,1,0:T(8,128)(2,1)S(1)}, u32[]{:S(2)}, u32[]{:S(2)}) %all-to-all-start.2) | async-done | bytes 491552 | tf_op jit(solution)/shard_map/all_to_all | solution.py:445
  102.5 0.9 pool.1
  (33 shorter events, 2.8 us)
Async XLA Ops:
  0.6 25.0 %copy-start.6 = (bf16[4096,256]{1,0:T(8,128)(2,1)S(1)}, bf16[4096,256]{1,0:T(8,128)(2,1)}, u32[]{:S(2)}) copy-start(bf16[4096,256]{1,0:T(8,128)(2,1)} %param.7) | copy-start | bytes 6291460
  3.3 44.5 %all-to-all-start = ((bf16[48,24,256]{2,1,0:T(8,128)(2,1)}), bf16[48,24,256]{2,1,0:T(8,128)(2,1)S(1)}, u32[]{:S(2)}, u32[]{:S(2)}) async-start(bf16[48,24,256]{2,1,0:T(8,128)(2,1)} %bitcast.24), calls=%async_computation | async-start | bytes 1179648 | tf_op jit(solution)/shard_map/all_to_all | solution.py:401
  25.6 5.7 %copy-start.7 = (f32[4096]{0:T(1024)S(1)}, f32[4096]{0:T(1024)}, u32[]{:S(2)}) copy-start(f32[4096]{0:T(1024)} %param.8) | copy-start | bytes 49156
  25.6 10.8 %copy-start.8 = (s32[1024]{0:T(1024)S(1)}, s32[1024]{0:T(1024)}, u32[]{:S(2)}) copy-start(s32[1024]{0:T(1024)} %param.9) | copy-start | bytes 12292
  38.6 24.0 %copy-start.4 = (s32[1,48,20]{1,0,2:T(1,128)S(1)}, s32[1,48,20]{1,0,2:T(1,128)}, u32[]{:S(2)}) copy-start(s32[1,48,20]{1,0,2:T(1,128)} %param.11) | copy-start | bytes 11524
  38.6 24.0 %copy-start.5 = (s32[1,48]{1,0:T(1,128)S(1)}, s32[1,48]{1,0:T(1,128)}, u32[]{:S(2)}) copy-start(s32[1,48]{1,0:T(1,128)} %counts_ref.3) | copy-start | bytes 580
  55.1 19.2 %all-to-all-start.1 = ((bf16[16,32,256]{2,1,0:T(8,128)(2,1)}), bf16[16,32,256]{2,1,0:T(8,128)(2,1)S(1)}, u32[]{:S(2)}, u32[]{:S(2)}) async-start(bf16[16,32,256]{2,1,0:T(8,128)(2,1)} %bitcast.25), calls=%async_computation.1 | async-start | bytes 524288 | tf_op jit(solution)/shard_map/all_to_all | solution.py:438
  63.0 0.8 copy-start.1
  63.8 1.0 %copy-start = (bf16[1024,256]{1,0:T(8,128)(2,1)S(1)}, bf16[1024,256]{1,0:T(8,128)(2,1)}, u32[]{:S(2)}) copy-start(bf16[1024,256]{1,0:T(8,128)(2,1)} %gather_fusion) | copy-start | bytes 1572868
  66.0 0.8 copy-start.3
  74.3 28.2 %all-to-all-start.2 = ((bf16[48,40,128]{2,1,0:T(8,128)(2,1)}), bf16[48,40,128]{2,1,0:T(8,128)(2,1)S(1)}, u32[]{:S(2)}, u32[]{:S(2)}) async-start(bf16[48,40,128]{2,1,0:T(8,128)(2,1)} %copy-done.3), calls=%async_computation.2 | async-start | bytes 983040 | tf_op jit(solution)/shard_map/all_to_all | solution.py:445
  79.3 23.2 %copy-start.2 = (bf16[128,1920]{1,0:T(8,128)(2,1)S(1)}, bf16[128,1920]{1,0:T(8,128)(2,1)}, u32[]{:S(2)}) copy-start(bf16[128,1920]{1,0:T(8,128)(2,1)} %copy-done.1) | copy-start | bytes 1474564

commit v5 on v4

--- a/solution.py
+++ b/solution.py
@@ -194,14 +194,28 @@
     return got
 
 
-def hits_kernel(capacity, got_ref, column_ref, theirs_ref, ours_ref, hits):
+def hits_kernel(
+    capacity, got_ref, column_ref, values_ref, theirs_ref, ours_ref, picked_ref, hits
+):
     got = hit_matrix(got_ref, column_ref, hits, capacity)
     half = theirs_ref.shape[0]
     theirs_ref[...] = dot(hits[0:half, :], got).astype(bf16)
     ours_ref[...] = dot(hits[half:, :], got)
-
-
-def partial_sums(got, column, capacity):
+    shards, pack, width = picked_ref.shape
+    whole = 16
+    rest = pack // 2 - whole
+    rows = dot_tn(hits[...], values_ref[...]).reshape(shards, block, 2 * width)
+    left, right = rows[:, :, 0:width], rows[:, :, width : 2 * width]
+    first = iota((shards, block - whole, width), 1) < rest
+    mixed = jnp.where(
+        first, left[:, whole:block, :], pltpu.roll(right[:, whole:block, :], rest, 1)
+    )
+    picked_ref[...] = jnp.concatenate(
+        [left[:, 0:whole, :], right[:, 0:whole, :], mixed], axis=1
+    ).astype(bf16)
+
+
+def sums_and_rows(got, column, values, shards, capacity):
     flat, width = got.shape
     touch = column.shape[0]
     return pl.pallas_call(
@@ -209,36 +223,11 @@
         out_shape=(
             jax.ShapeDtypeStruct((touch // 2, width), bf16),
             jax.ShapeDtypeStruct((touch // 2, width), f32),
+            jax.ShapeDtypeStruct((shards, 2 * capacity, width // 2), bf16),
         ),
         scratch_shapes=[pltpu.VMEM((touch, flat), bf16)],
         compiler_params=params,
         name="hits",
-    )(got, column)
-
-
-def pick_kernel(capacity, got_ref, column_ref, values_ref, out_ref, hits):
-    hit_matrix(got_ref, column_ref, hits, capacity)
-    shards, pack, half = out_ref.shape
-    whole = 16
-    rest = pack // 2 - whole
-    rows = dot_tn(hits[...], values_ref[...]).reshape(shards, block, 2 * half)
-    left, right = rows[:, :, 0:half], rows[:, :, half : 2 * half]
-    first = iota((shards, block - whole, half), 1) < rest
-    mixed = jnp.where(
-        first, left[:, whole:block, :], pltpu.roll(right[:, whole:block, :], rest, 1)
-    )
-    out_ref[...] = jnp.concatenate(
-        [left[:, 0:whole, :], right[:, 0:whole, :], mixed], axis=1
-    ).astype(bf16)
-
-
-def pick_rows(got, column, values, shards, capacity):
-    return pl.pallas_call(
-        functools.partial(pick_kernel, capacity),
-        out_shape=jax.ShapeDtypeStruct((shards, 2 * capacity, values.shape[1] // 2), bf16),
-        scratch_shapes=[pltpu.VMEM((values.shape[0], got.shape[0]), bf16)],
-        compiler_params=params,
-        name="pick",
     )(got, column, values)
 
 
@@ -417,20 +406,26 @@
     chunk = mine // 2
     mine_rows = lax.dynamic_slice(order.reshape(2, half), (0, replica * chunk), (2, chunk))
     mine_rows = mine_rows.reshape(mine)
-    mine_values = jnp.take(table, mine_rows, axis=0, mode="clip")
+    mine_values = jnp.concatenate(
+        [
+            lax.dynamic_slice(values, ((1 - core) * half + replica * chunk, 0), (chunk, width)),
+            lax.dynamic_slice(values, (core * half + replica * chunk, 0), (chunk, width)),
+        ]
+    )
     mine_state = jnp.take(row_state, mine_rows, mode="clip")[:, None]
     marked = jnp.zeros(row_state.shape, f32).at[touched_rows].set(
         1.0, mode="promise_in_bounds", unique_indices=True
     )
     kept_state = jnp.where(marked > 0, 0.0, row_state)
     kept_table = jnp.where(marked[:, None] > 0, jnp.zeros((), bf16), table)
-    got, column, values, kept_state, kept_table, mine_state, mine_values, starts = (
+    member = member_matrix(bags, route_counts)
+    got, column, values, kept_state, kept_table, mine_state, mine_values, starts, member = (
         lax.optimization_barrier(
-            (got, column, values, kept_state, kept_table, mine_state, mine_values, starts)
+            (got, column, values, kept_state, kept_table, mine_state, mine_values, starts, member)
         )
     )
 
-    theirs, ours = partial_sums(got, column, capacity)
+    theirs, ours, picked = sums_and_rows(got, column, values, shards, capacity)
     pairs = [[k, k + 1] for k in range(0, replicas, 2)]
     both = lax.all_gather(theirs, "replica", axis=0, tiled=True, axis_index_groups=pairs)
     theirs = lax.dynamic_slice(both, ((1 - core) * half, 0), (half, width))
@@ -438,10 +433,8 @@
     parts = lax.all_to_all(
         part.reshape(replicas, chunk, width), "replica", split_axis=0, concat_axis=0, tiled=True
     )
-    picked = pick_rows(got, column, values, shards, capacity)
-    member = member_matrix(bags, route_counts)
     offset = (lax.rem(replica, width // chunk) * chunk).astype(jnp.int32).reshape(1)
-    picked, member, parts = lax.optimization_barrier((picked, member, parts))
+    picked, parts = lax.optimization_barrier((picked, parts))
     returned = lax.all_to_all(picked, "shard", split_axis=0, concat_axis=0, tiled=True)
     updated = update_rows(offset, parts, mine_values, mine_state)
     every = lax.all_gather(updated, "replica", axis=0, tiled=True)

time: 104 us -> 104 us (level)
  blocking collectives: 21.5 us -> 40.4 us
  waiting for transfers between devices: 20 us -> 11.5 us
  starting transfers between devices: 31.3 us -> 23.8 us
  local copies, waits for them, and re-layouts: 14.6 us -> 12.5 us
    all_to_all x0 -> x1, blocking collectives: none -> 19 us  [local(): lax.all_to_all(part.reshape(replicas, chunk, width), 'replica', split_axi...]
    all_to_all x1 -> x0, waiting for transfers between devices: 7.55 us -> none  [local(): lax.all_to_all(part.reshape(replicas, chunk, width), 'replica', split_axi...]
    all_to_all x1 -> x0, starting transfers between devices: 7.49 us -> none  [local(): lax.all_to_all(part.reshape(replicas, chunk, width), 'replica', split_axi...]
    unnamed x18 -> x14, local copies, waits for them, and re-layouts: 2.61 us -> 0.81 us
    pallas_call x2 -> x1, Pallas kernels: 2.25 us -> 1.85 us  [sums_and_rows(): pl.pallas_call(functools.partial(hits_kernel, capacity), out_shape=(jax.S...]
  transfers between devices with their start and end apart: 3 -> 2, of which waited for: 3 -> 2; matrix products, arithmetic and copies ran while one was open for 15% -> 15% of each run, Pallas kernels for 6% -> 5%
where the time goes in v5:
time: 104 us; the launch traced here: 103 us
  blocking collectives  40.4 us (39%)
  starting transfers between devices  23.8 us (23%)
  local copies, waits for them, and re-layouts  12.5 us (12%)
  waiting for transfers between devices  11.5 us (11%)
  Pallas kernels  10.3 us (10%)
  other arithmetic  3.64 us (4%)
    all_to_all x1, blocking collectives, local(): lax.all_to_all(part.reshape(replicas, chunk, width), 'replica', split_axi...  19 us
    all_to_all x1, starting transfers between devices, local(): lax.all_to_all(send.reshape(shards, block, width), 'shard', split_axis=0,...  18.9 us
    all_gather x1, blocking collectives, local(): every = lax.all_gather(updated, 'replica', axis=0, tiled=True)  16.3 us
    all_to_all x1, waiting for transfers between devices, local(): lax.all_to_all(send.reshape(shards, block, width), 'shard', split_axis=0,...  8.34 us
    gather x1, local copies, waits for them, and re-layouts, local(): values = jnp.take(table, turned, axis=0, mode='clip')  5.35 us
    all_gather x1, blocking collectives, local(): lax.all_gather(theirs, 'replica', axis=0, tiled=True, axis_index_groups=p...  5.18 us
    all_to_all x1, starting transfers between devices, local(): lax.all_to_all(picked, 'shard', split_axis=0, concat_axis=0, tiled=True)  4.94 us
    scatter x1, local copies, waits for them, and re-layouts, local(): jnp.zeros(row_state.shape, f32).at[touched_rows]  4.33 us
  transfers between devices with their start and end apart: 2, of which 2 were waited for; matrix products, arithmetic and copies ran while one was open for 15% of the time, Pallas kernels for 5%

profile of v5, /device:TPU:1, one launch (start us, length us, event | category | flops | bytes accessed | tf_op | source)
XLA Modules:
  0.0 103.1 jit_solution(8404661476516558505)
XLA Ops:
  0.7 2.5 %prep.1 = bf16[1152,256]{1,0:T(8,128)(2,1)} custom-call(s32[20,1,48]{2,1,0:T(1,128)} %bitcast.25, s32[20,1,48]{2,1,0:T(1,128)} %bitcast.19, s32[1,48]{1,0:T(1,128)} %counts_ref.3, f32[40,256]{1,0:T(8,128)} %grad_ref.1), custom_call_target="tpu_custom_call" | custom-call | tf_op jit(solution)/shard_map/prep/pallas_call | solution.py:90
  3.2 18.9 %all-to-all-start = ((bf16[48,24,256]{2,1,0:T(8,128)(2,1)}), bf16[48,24,256]{2,1,0:T(8,128)(2,1)S(1)}, u32[]{:S(2)}, u32[]{:S(2)}) async-start(bf16[48,24,256]{2,1,0:T(8,128)(2,1)} %bitcast.23), calls=%async_computation | async-start | bytes 1179648 | tf_op jit(solution)/shard_map/all_to_all | solution.py:390
  22.0 0.8 compare_select_fusion
  22.8 0.2 copy.13.column_ref
  23.0 1.0 sort.1.listed_ref
  24.1 0.5 broadcast.31
  24.6 0.7 reduce.3
  25.5 0.4 member.1.member_ref
  25.9 0.8 copy-done
  26.7 5.3 %gather_fusion = bf16[1024,256]{1,0:T(8,128)(2,1)S(1)} fusion(bf16[4096,256]{1,0:T(8,128)(2,1)} %param.7, s32[1024]{0:T(1024)S(1)} %get-tuple-element.41), kind=kCustom, calls=%fused_computation | custom fusion | bytes 1052672 | tf_op jit(solution)/shard_map/jit(_take)/gather | solution.py:405
  32.1 0.8 gather_fusion.1
  32.8 4.3 %scatter_custom_fusion = f32[4096]{0:T(1024)S(1)} fusion(s32[1024]{0:T(1024)S(1)} %get-tuple-element.39, f32[1024]{0:T(1024)S(1)} %broadcast.15, f32[]{:T(128)} %constant.9.clone.1), kind=kCustom, calls=%fused_computation.10 | custom fusion | bytes 16388 | tf_op jit(solution)/shard_map/scatter | solution.py:416
  37.2 0.2 convert_reduce_fusion.starts
  37.4 1.9 %broadcast_select_fusion.table_ref = bf16[4096,256]{1,0:T(8,128)(2,1)S(1)} fusion(bf16[4096,256]{1,0:T(8,128)(2,1)} %param.7, pred[4096]{0:T(1024)(128)(4,1)S(1)} %get-tuple-element.36), kind=kLoop, calls=%fused_computation.3 | loop fusion | flops 1048576 | bytes 4198400 | tf_op jit(solution)/shard_map/jit(_where)/select_n | solution.py:420
  39.4 8.3 %all-to-all-done = bf16[48,24,256]{2,1,0:T(8,128)(2,1)S(1)} async-done(((bf16[48,24,256]{2,1,0:T(8,128)(2,1)}), bf16[48,24,256]{2,1,0:T(8,128)(2,1)S(1)}, u32[]{:S(2)}, u32[]{:S(2)}) %all-to-all-start) | async-done | bytes 589856 | tf_op jit(solution)/shard_map/all_to_all | solution.py:390
  47.9 1.9 %hits.1 = (bf16[512,256]{1,0:T(8,128)(2,1)S(1)}, f32[512,256]{1,0:T(8,128)S(1)}, bf16[48,40,128]{2,1,0:T(8,128)(2,1)S(1)}) custom-call(bf16[1152,256]{1,0:T(8,128)(2,1)S(1)} %bitcast.15, f32[1024,128]{1,0:T(8,128)S(1)} %broadcast_in_dim.37.column_ref, bf16[1024,256]{1,0:T(8,128)(2,1)S(1)} %gather_fusion), custom_call_target="tpu_custom_call" | custom-call | tf_op jit(solution)/shard_map/hits/pallas_call | solution.py:221
  49.8 5.2 %all_gather.6 = bf16[1024,256]{1,0:T(8,128)(2,1)S(1)} all-gather(bf16[512,256]{1,0:T(8,128)(2,1)S(1)} %get-tuple-element.25), channel_id=1, replica_groups={{0,48},{96,144},{192,240},{288,336},{384,432},{480,528},{576,624},{672,..., dimensions={0}, use_global_device_ids=true | all-gather | bytes 786432 | tf_op jit(solution)/shard_map/all_gather | solution.py:430
  55.0 19.0 %all_to_all.15.parts_ref = bf16[16,32,256]{2,1,0:T(8,128)(2,1)S(1)} all-to-all(bf16[16,32,256]{2,1,0:T(8,128)(2,1)S(1)} %bitcast.24), channel_id=1, replica_groups=mesh['replica'=16,'shard'=48] {'replica'}, dimensions={0} | all-to-all | bytes 524288 | tf_op jit(solution)/shard_map/all_to_all | solution.py:433
  74.0 4.9 %all-to-all-start.2 = ((bf16[48,40,128]{2,1,0:T(8,128)(2,1)}), bf16[48,40,128]{2,1,0:T(8,128)(2,1)S(1)}, u32[]{:S(2)}, u32[]{:S(2)}) async-start(bf16[48,40,128]{2,1,0:T(8,128)(2,1)} %copy-done.2), calls=%async_computation.2 | async-start | bytes 983040 | tf_op jit(solution)/shard_map/all_to_all | solution.py:438
  79.1 0.2 update.1
  79.3 16.3 %all_gather.7.every_ref = bf16[1280,256]{1,0:T(8,128)(2,1)S(1)} all-gather(bf16[80,256]{1,0:T(8,128)(2,1)S(1)} %update.1), channel_id=1, replica_groups=mesh['replica'=16,'shard'=48] {'replica'}, dimensions={0}, use_global_device_ids=true | all-gather | bytes 696320 | tf_op jit(solution)/shard_map/all_gather | solution.py:440
  95.6 3.4 %place.1 = (bf16[4096,256]{1,0:T(8,128)(2,1)}, f32[32,128]{1,0:T(8,128)}) custom-call(s32[32]{0:T(128)S(1)} %convert_reduce_fusion.starts, bf16[1280,256]{1,0:T(8,128)(2,1)S(1)} %all_gather.7.every_ref, s32[1,1024]{1,0:T(1,128)S(1)} %sort.1.listed_ref, s32[16,128]{1,0:T(8,128)S(1)} %pad.4.tiles_ref, bf16[4096,256]{1,0:T(8,128)(2,1)S(1)} %broadcast_select_fusion.table_ref, ...), custom_call_target="tpu_custom_call" | custom-call | tf_op jit(solution)/shard_map/place/pallas_call | solution.py:336
  99.0 3.2 %all-to-all-done.2 = bf16[48,40,128]{2,1,0:T(8,128)(2,1)S(1)} async-done(((bf16[48,40,128]{2,1,0:T(8,128)(2,1)}), bf16[48,40,128]{2,1,0:T(8,128)(2,1)S(1)}, u32[]{:S(2)}, u32[]{:S(2)}) %all-to-all-start.2) | async-done | bytes 491552 | tf_op jit(solution)/shard_map/all_to_all | solution.py:438
  102.2 0.9 pool.1
  (28 shorter events, 0.6 us)
Async XLA Ops:
  0.6 24.8 %copy-start.3 = (s32[1,48,20]{1,0,2:T(1,128)S(1)}, s32[1,48,20]{1,0,2:T(1,128)}, u32[]{:S(2)}) copy-start(s32[1,48,20]{1,0,2:T(1,128)} %param.11) | copy-start | bytes 11524
  0.6 24.8 %copy-start.4 = (s32[1,48]{1,0:T(1,128)S(1)}, s32[1,48]{1,0:T(1,128)}, u32[]{:S(2)}) copy-start(s32[1,48]{1,0:T(1,128)} %counts_ref.3) | copy-start | bytes 580
  3.2 44.6 %all-to-all-start = ((bf16[48,24,256]{2,1,0:T(8,128)(2,1)}), bf16[48,24,256]{2,1,0:T(8,128)(2,1)S(1)}, u32[]{:S(2)}, u32[]{:S(2)}) async-start(bf16[48,24,256]{2,1,0:T(8,128)(2,1)} %bitcast.23), calls=%async_computation | async-start | bytes 1179648 | tf_op jit(solution)/shard_map/all_to_all | solution.py:390
  25.9 0.8 copy-start
  26.7 5.4 %copy-start.5 = (f32[4096]{0:T(1024)S(1)}, f32[4096]{0:T(1024)}, u32[]{:S(2)}) copy-start(f32[4096]{0:T(1024)} %param.8) | copy-start | bytes 49156
  26.7 10.5 %copy-start.6 = (s32[1024]{0:T(1024)S(1)}, s32[1024]{0:T(1024)}, u32[]{:S(2)}) copy-start(s32[1024]{0:T(1024)} %param.9) | copy-start | bytes 12292
  49.8 24.2 %copy-start.2 = (bf16[48,40,128]{2,1,0:T(8,128)(2,1)}, bf16[48,40,128]{2,1,0:T(8,128)(2,1)S(1)}, u32[]{:S(2)}) copy-start(bf16[48,40,128]{2,1,0:T(8,128)(2,1)S(1)} %get-tuple-element.26) | copy-start | bytes 1474564
  74.0 28.2 %all-to-all-start.2 = ((bf16[48,40,128]{2,1,0:T(8,128)(2,1)}), bf16[48,40,128]{2,1,0:T(8,128)(2,1)S(1)}, u32[]{:S(2)}, u32[]{:S(2)}) async-start(bf16[48,40,128]{2,1,0:T(8,128)(2,1)} %copy-done.2), calls=%async_computation.2 | async-start | bytes 983040 | tf_op jit(solution)/shard_map/all_to_all | solution.py:438
  79.0 23.2 %copy-start.1 = (bf16[128,1920]{1,0:T(8,128)(2,1)S(1)}, bf16[128,1920]{1,0:T(8,128)(2,1)}, u32[]{:S(2)}) copy-start(bf16[128,1920]{1,0:T(8,128)(2,1)} %copy-done) | copy-start | bytes 1474564

commit v6 on v5

--- a/solution.py
+++ b/solution.py
@@ -49,6 +49,7 @@
     capacity, _, shards = rows_ref.shape
     bag_count, width = grad_ref.shape
     flat = shards * block
+    groups = held.shape[1]
     key = keys_of(bags_ref, counts_ref)
     position, lane = iota((flat, 128), 0), iota((flat, 128), 1)
     pair = pair_of(position)
@@ -68,7 +69,7 @@
     lane = iota((width, capacity), 0)
     sub = iota((width, capacity), 1)
     meta = dot(jnp.where(lane == sub, 1.0, 0.0).astype(bf16), high) + dot(
-        jnp.where(lane == sub + 128, 1.0, 0.0).astype(bf16), low
+        jnp.where(lane == sub + 64, 1.0, 0.0).astype(bf16), low
     )
     at_meta = jnp.where(slot == capacity, spread, 0.0).astype(bf16)[:, 0:shards]
     meta = meta.astype(bf16)
@@ -77,8 +78,15 @@
     copies = []
     for k in range(pieces):
         here = slice(k * size, (k + 1) * size)
-        held[here, :] = (dot(member[here], grads) + dot_nt(at_meta[here], meta)).astype(bf16)
-        at = pl.ds(k * size, size)
+        rows = dot(member[here], grads) + dot_nt(at_meta[here], meta)
+        pairs = shards // pieces
+        rows = rows.reshape(pairs, block, width)
+        to = slice(k * pairs, (k + 1) * pairs)
+        for g in range(groups - 1):
+            q, h = g // 2, (g % 2) * 128
+            held[to, g] = rows[:, 4 * q : 4 * q + 4, h : h + 128].astype(bf16)
+        held[to, groups - 1] = rows[:, capacity : capacity + 4, 0:128].astype(bf16)
+        at = pl.ds(k * pairs, pairs)
         copies.append(pltpu.make_async_copy(held.at[at], out_ref.at[at], sems.at[k]))
         copies[-1].start()
     for copy in copies:
@@ -86,15 +94,13 @@
 
 
 def prep(rows, bags, counts, grad):
-    shards = rows.shape[2]
+    capacity, _, shards = rows.shape
+    shape = (shards, capacity // 2 + 1, 4, 128)
     return pl.pallas_call(
         prep_kernel,
-        out_shape=jax.ShapeDtypeStruct((shards * block, grad.shape[1]), bf16),
+        out_shape=jax.ShapeDtypeStruct(shape, bf16),
         out_specs=pl.BlockSpec(memory_space=pltpu.HBM),
-        scratch_shapes=[
-            pltpu.VMEM((shards * block, grad.shape[1]), bf16),
-            pltpu.SemaphoreType.DMA((4,)),
-        ],
+        scratch_shapes=[pltpu.VMEM(shape, bf16), pltpu.SemaphoreType.DMA((4,))],
         compiler_params=large,
         name="prep",
     )(rows, bags, counts, grad)
@@ -176,15 +182,22 @@
 
 
 def hit_matrix(got_ref, column_ref, hits, capacity):
-    flat, width = got_ref.shape
-    shards = flat // block
+    shards, groups, _, half = got_ref.shape
+    flat = shards * block
+    left = [got_ref[:, g].astype(f32) for g in range(0, groups - 1, 2)]
+    right = [got_ref[:, g].astype(f32) for g in range(1, groups - 1, 2)]
+    meta = got_ref[:, groups - 1].astype(f32)
+    none = jnp.zeros(meta.shape, f32)
+    got = jnp.concatenate(
+        [jnp.concatenate(left + [none], axis=1), jnp.concatenate(right + [none], axis=1)], axis=2
+    )
+    got = got.reshape(flat, 2 * half).astype(bf16)
     column = column_ref[...]
-    got = got_ref[...]
-    meta = got.astype(f32).reshape(shards, block, width)[:, capacity : capacity + 1, :]
-    shape = (shards, block, width)
-    own = (iota(shape, 2) & 127) == iota(shape, 1)
-    spread = jnp.where(own, jnp.broadcast_to(meta, shape), 0.0).reshape(flat, width).astype(bf16)
-    weigh = jnp.where(iota((8, width), 1) < 128, 64.0, 1.0).astype(bf16)
+    shape = (shards, block, half)
+    own = (iota(shape, 2) & 63) == iota(shape, 1)
+    spread = jnp.where(own, jnp.broadcast_to(meta[:, 0:1, :], shape), 0.0)
+    spread = spread.reshape(flat, half).astype(bf16)
+    weigh = jnp.where(iota((8, half), 1) < 64, 64.0, 1.0).astype(bf16)
     rows = dot_nt(weigh, spread)
     lane = iota((8, flat), 1)
     rows = jnp.where(lane - block * pair_of(lane) < capacity, rows, -1.0)
@@ -216,7 +229,7 @@
 
 
 def sums_and_rows(got, column, values, shards, capacity):
-    flat, width = got.shape
+    flat, width = shards * block, values.shape[1]
     touch = column.shape[0]
     return pl.pallas_call(
         functools.partial(hits_kernel, capacity),
@@ -387,9 +400,7 @@
 
     bags = jnp.transpose(lookup_bags, (2, 0, 1))
     send = prep(jnp.transpose(lookup_rows, (2, 0, 1)), bags, route_counts, pooled_grad)
-    got = lax.all_to_all(
-        send.reshape(shards, block, width), "shard", split_axis=0, concat_axis=0, tiled=True
-    ).reshape(shards * block, width)
+    got = lax.all_to_all(send, "shard", split_axis=0, concat_axis=0, tiled=True)
 
     listed = sort_list(touched_rows)
     replica = lax.axis_index("replica")

time: 104 us -> 102 us (0.981)
  waiting for transfers between devices: 11.5 us -> 9.91 us
    all_to_all x1, waiting for transfers between devices: 8.34 us -> 6.74 us  [local(): got = lax.all_to_all(send, 'shard', split_axis=0, concat_axis=0, tiled=True)]
where the time goes in v6:
time: 102 us
  blocking collectives  40.4 us (40%)
  starting transfers between devices  23.8 us (23%)
  local copies, waits for them, and re-layouts  12.5 us (12%)
  Pallas kernels  10.4 us (10%)
  waiting for transfers between devices  9.91 us (10%)
  other arithmetic  3.64 us (4%)
    all_to_all x1, blocking collectives, local(): lax.all_to_all(part.reshape(replicas, chunk, width), 'replica', split_axi...  19 us
    all_to_all x1, starting transfers between devices, local(): got = lax.all_to_all(send, 'shard', split_axis=0, concat_axis=0, tiled=True)  18.9 us
    all_gather x1, blocking collectives, local(): every = lax.all_gather(updated, 'replica', axis=0, tiled=True)  16.3 us
    all_to_all x1, waiting for transfers between devices, local(): got = lax.all_to_all(send, 'shard', split_axis=0, concat_axis=0, tiled=True)  6.74 us
    gather x1, local copies, waits for them, and re-layouts, local(): values = jnp.take(table, turned, axis=0, mode='clip')  5.35 us
    all_gather x1, blocking collectives, local(): lax.all_gather(theirs, 'replica', axis=0, tiled=True, axis_index_groups=p...  5.15 us
    all_to_all x1, starting transfers between devices, local(): lax.all_to_all(picked, 'shard', split_axis=0, concat_axis=0, tiled=True)  5 us
    scatter x1, local copies, waits for them, and re-layouts, local(): jnp.zeros(row_state.shape, f32).at[touched_rows]  4.33 us
  transfers between devices with their start and end apart: 2, of which 2 were waited for; matrix products, arithmetic and copies ran while one was open for 15% of the time, Pallas kernels for 5%

profile of v6, /device:TPU:1, one launch (start us, length us, event | category | flops | bytes accessed | tf_op | source)
XLA Modules:
  0.0 101.6 jit_solution(14190481360898689123)
XLA Ops:
  0.7 2.5 %prep.1 = bf16[48,11,4,128]{3,2,1,0:T(4,128)(2,1)} custom-call(s32[20,1,48]{2,1,0:T(1,128)} %bitcast.21, s32[20,1,48]{2,1,0:T(1,128)} %bitcast.16, s32[1,48]{1,0:T(1,128)} %counts_ref.3, f32[40,256]{1,0:T(8,128)} %grad_ref.1), custom_call_target="tpu_custom_call" | custom-call | tf_op jit(solution)/shard_map/prep/pallas_call | solution.py:99
  3.2 18.9 %all-to-all-start = ((bf16[48,11,4,128]{3,2,1,0:T(4,128)(2,1)}), bf16[48,11,4,128]{3,2,1,0:T(4,128)(2,1)S(1)}, u32[]{:S(2)}, u32[]{:S(2)}) async-start(bf16[48,11,4,128]{3,2,1,0:T(4,128)(2,1)} %prep.1), calls=%async_computation | async-start | bytes 1081344 | tf_op jit(solution)/shard_map/all_to_all | solution.py:403
  22.1 0.8 compare_select_fusion
  22.8 0.2 copy.13.column_ref
  23.1 1.0 %sort.1.listed_ref = s32[1,1024]{1,0:T(1,128)S(1)} custom-call(f32[1,1024]{1,0:T(1,128)S(1)} %bitcast.19, f32[1024,1]{1,0:T(8,128)S(1)} %copy.13.column_ref), custom_call_target="tpu_custom_call" | custom-call | tf_op jit(solution)/shard_map/sort/pallas_call | solution.py:176
  24.1 0.5 broadcast.31
  24.6 0.7 reduce.3
  25.5 0.4 member.1.member_ref
  25.9 0.8 copy-done
  26.7 5.3 %gather_fusion = bf16[1024,256]{1,0:T(8,128)(2,1)S(1)} fusion(bf16[4096,256]{1,0:T(8,128)(2,1)} %param.7, s32[1024]{0:T(1024)S(1)} %get-tuple-element.41), kind=kCustom, calls=%fused_computation | custom fusion | bytes 1052672 | tf_op jit(solution)/shard_map/jit(_take)/gather | solution.py:416
  32.1 0.8 gather_fusion.1
  32.9 4.3 %scatter_custom_fusion = f32[4096]{0:T(1024)S(1)} fusion(s32[1024]{0:T(1024)S(1)} %get-tuple-element.39, f32[1024]{0:T(1024)S(1)} %broadcast.15, f32[]{:T(128)} %constant.9.clone.1), kind=kCustom, calls=%fused_computation.10 | custom fusion | bytes 16388 | tf_op jit(solution)/shard_map/scatter | solution.py:427
  37.2 0.2 convert_reduce_fusion.starts
  37.4 1.9 %broadcast_select_fusion.table_ref = bf16[4096,256]{1,0:T(8,128)(2,1)S(1)} fusion(bf16[4096,256]{1,0:T(8,128)(2,1)} %param.7, pred[4096]{0:T(1024)(128)(4,1)S(1)} %get-tuple-element.36), kind=kLoop, calls=%fused_computation.3 | loop fusion | flops 1048576 | bytes 4198400 | tf_op jit(solution)/shard_map/jit(_where)/select_n | solution.py:431
  39.4 6.7 %all-to-all-done.got_ref = bf16[48,11,4,128]{3,2,1,0:T(4,128)(2,1)S(1)} async-done(((bf16[48,11,4,128]{3,2,1,0:T(4,128)(2,1)}), bf16[48,11,4,128]{3,2,1,0:T(4,128)(2,1)S(1)}, u32[]{:S(2)}, u32[]{:S(2)}) %all-to-all-start) | async-done | bytes 540704 | tf_op jit(solution)/shard_map/all_to_all | solution.py:403
  46.3 1.9 %hits.1 = (bf16[512,256]{1,0:T(8,128)(2,1)S(1)}, f32[512,256]{1,0:T(8,128)S(1)}, bf16[48,40,128]{2,1,0:T(8,128)(2,1)S(1)}) custom-call(bf16[48,11,4,128]{3,2,1,0:T(4,128)(2,1)S(1)} %all-to-all-done.got_ref, f32[1024,128]{1,0:T(8,128)S(1)} %broadcast_in_dim.37.column_ref, bf16[1024,256]{1,0:T(8,128)(2,1)S(1)} %gather_fusion), custom_call_target="tpu_custom_call" | custom-call | tf_op jit(solution)/shard_map/hits/pallas_call | solution.py:234
  48.2 5.2 %all_gather.6 = bf16[1024,256]{1,0:T(8,128)(2,1)S(1)} all-gather(bf16[512,256]{1,0:T(8,128)(2,1)S(1)} %get-tuple-element.25), channel_id=1, replica_groups={{0,48},{96,144},{192,240},{288,336},{384,432},{480,528},{576,624},{672,..., dimensions={0}, use_global_device_ids=true | all-gather | bytes 786432 | tf_op jit(solution)/shard_map/all_gather | solution.py:441
  53.4 19.0 %all_to_all.15.parts_ref = bf16[16,32,256]{2,1,0:T(8,128)(2,1)S(1)} all-to-all(bf16[16,32,256]{2,1,0:T(8,128)(2,1)S(1)} %bitcast.20), channel_id=1, replica_groups=mesh['replica'=16,'shard'=48] {'replica'}, dimensions={0} | all-to-all | bytes 524288 | tf_op jit(solution)/shard_map/all_to_all | solution.py:444
  72.4 5.0 %all-to-all-start.2 = ((bf16[48,40,128]{2,1,0:T(8,128)(2,1)}), bf16[48,40,128]{2,1,0:T(8,128)(2,1)S(1)}, u32[]{:S(2)}, u32[]{:S(2)}) async-start(bf16[48,40,128]{2,1,0:T(8,128)(2,1)} %copy-done.2), calls=%async_computation.2 | async-start | bytes 983040 | tf_op jit(solution)/shard_map/all_to_all | solution.py:449
  77.6 0.2 update.1
  77.8 16.3 %all_gather.7.every_ref = bf16[1280,256]{1,0:T(8,128)(2,1)S(1)} all-gather(bf16[80,256]{1,0:T(8,128)(2,1)S(1)} %update.1), channel_id=1, replica_groups=mesh['replica'=16,'shard'=48] {'replica'}, dimensions={0}, use_global_device_ids=true | all-gather | bytes 696320 | tf_op jit(solution)/shard_map/all_gather | solution.py:451
  94.1 3.4 %place.1 = (bf16[4096,256]{1,0:T(8,128)(2,1)}, f32[32,128]{1,0:T(8,128)}) custom-call(s32[32]{0:T(128)S(1)} %convert_reduce_fusion.starts, bf16[1280,256]{1,0:T(8,128)(2,1)S(1)} %all_gather.7.every_ref, s32[1,1024]{1,0:T(1,128)S(1)} %sort.1.listed_ref, s32[16,128]{1,0:T(8,128)S(1)} %pad.4.tiles_ref, bf16[4096,256]{1,0:T(8,128)(2,1)S(1)} %broadcast_select_fusion.table_ref, ...), custom_call_target="tpu_custom_call" | custom-call | tf_op jit(solution)/shard_map/place/pallas_call | solution.py:349
  97.5 3.2 %all-to-all-done.2 = bf16[48,40,128]{2,1,0:T(8,128)(2,1)S(1)} async-done(((bf16[48,40,128]{2,1,0:T(8,128)(2,1)}), bf16[48,40,128]{2,1,0:T(8,128)(2,1)S(1)}, u32[]{:S(2)}, u32[]{:S(2)}) %all-to-all-start.2) | async-done | bytes 491552 | tf_op jit(solution)/shard_map/all_to_all | solution.py:449
  100.6 0.9 pool.1
  (28 shorter events, 0.6 us)
Async XLA Ops:
  0.6 24.9 %copy-start.3 = (s32[1,48,20]{1,0,2:T(1,128)S(1)}, s32[1,48,20]{1,0,2:T(1,128)}, u32[]{:S(2)}) copy-start(s32[1,48,20]{1,0,2:T(1,128)} %param.11) | copy-start | bytes 11524
  0.6 24.9 %copy-start.4 = (s32[1,48]{1,0:T(1,128)S(1)}, s32[1,48]{1,0:T(1,128)}, u32[]{:S(2)}) copy-start(s32[1,48]{1,0:T(1,128)} %counts_ref.3) | copy-start | bytes 580
  3.2 42.9 %all-to-all-start = ((bf16[48,11,4,128]{3,2,1,0:T(4,128)(2,1)}), bf16[48,11,4,128]{3,2,1,0:T(4,128)(2,1)S(1)}, u32[]{:S(2)}, u32[]{:S(2)}) async-start(bf16[48,11,4,128]{3,2,1,0:T(4,128)(2,1)} %prep.1), calls=%async_computation | async-start | bytes 1081344 | tf_op jit(solution)/shard_map/all_to_all | solution.py:403
  25.9 0.8 copy-start
  26.7 5.4 %copy-start.5 = (f32[4096]{0:T(1024)S(1)}, f32[4096]{0:T(1024)}, u32[]{:S(2)}) copy-start(f32[4096]{0:T(1024)} %param.8) | copy-start | bytes 49156
  26.7 10.5 %copy-start.6 = (s32[1024]{0:T(1024)S(1)}, s32[1024]{0:T(1024)}, u32[]{:S(2)}) copy-start(s32[1024]{0:T(1024)} %param.9) | copy-start | bytes 12292
  48.2 24.2 %copy-start.2 = (bf16[48,40,128]{2,1,0:T(8,128)(2,1)}, bf16[48,40,128]{2,1,0:T(8,128)(2,1)S(1)}, u32[]{:S(2)}) copy-start(bf16[48,40,128]{2,1,0:T(8,128)(2,1)S(1)} %get-tuple-element.26) | copy-start | bytes 1474564
  72.4 28.2 %all-to-all-start.2 = ((bf16[48,40,128]{2,1,0:T(8,128)(2,1)}), bf16[48,40,128]{2,1,0:T(8,128)(2,1)S(1)}, u32[]{:S(2)}, u32[]{:S(2)}) async-start(bf16[48,40,128]{2,1,0:T(8,128)(2,1)} %copy-done.2), calls=%async_computation.2 | async-start | bytes 983040 | tf_op jit(solution)/shard_map/all_to_all | solution.py:449
  77.4 23.2 %copy-start.1 = (bf16[128,1920]{1,0:T(8,128)(2,1)S(1)}, bf16[128,1920]{1,0:T(8,128)(2,1)}, u32[]{:S(2)}) copy-start(bf16[128,1920]{1,0:T(8,128)(2,1)} %copy-done) | copy-start | bytes 1474564

commit v7 on v6

--- a/solution.py
+++ b/solution.py
@@ -84,8 +84,8 @@
         to = slice(k * pairs, (k + 1) * pairs)
         for g in range(groups - 1):
             q, h = g // 2, (g % 2) * 128
-            held[to, g] = rows[:, 4 * q : 4 * q + 4, h : h + 128].astype(bf16)
-        held[to, groups - 1] = rows[:, capacity : capacity + 4, 0:128].astype(bf16)
+            held[to, g] = rows[:, 2 * q : 2 * q + 2, h : h + 128].astype(bf16)
+        held[to, groups - 1] = rows[:, capacity : capacity + 2, 0:128].astype(bf16)
         at = pl.ds(k * pairs, pairs)
         copies.append(pltpu.make_async_copy(held.at[at], out_ref.at[at], sems.at[k]))
         copies[-1].start()
@@ -95,7 +95,7 @@
 
 def prep(rows, bags, counts, grad):
     capacity, _, shards = rows.shape
-    shape = (shards, capacity // 2 + 1, 4, 128)
+    shape = (shards, capacity + 1, 2, 128)
     return pl.pallas_call(
         prep_kernel,
         out_shape=jax.ShapeDtypeStruct(shape, bf16),
@@ -187,7 +187,7 @@
     left = [got_ref[:, g].astype(f32) for g in range(0, groups - 1, 2)]
     right = [got_ref[:, g].astype(f32) for g in range(1, groups - 1, 2)]
     meta = got_ref[:, groups - 1].astype(f32)
-    none = jnp.zeros(meta.shape, f32)
+    none = jnp.zeros((shards, block - capacity, half), f32)
     got = jnp.concatenate(
         [jnp.concatenate(left + [none], axis=1), jnp.concatenate(right + [none], axis=1)], axis=2
     )

time: 102 us -> 102 us (level)
  waiting for transfers between devices: 9.91 us -> 8.34 us
  local copies, waits for them, and re-layouts: 12.5 us -> 13.8 us
    all_to_all x1, waiting for transfers between devices: 6.74 us -> 5.17 us  [local(): got = lax.all_to_all(send, 'shard', split_axis=0, concat_axis=0, tiled=True)]
    unnamed x14, local copies, waits for them, and re-layouts: 0.81 us -> 2.16 us
  transfers between devices with their start and end apart: 2 -> 2, of which waited for: 2 -> 2; matrix products, arithmetic and copies ran while one was open for 15% -> 14% of each run, Pallas kernels for 5% -> 5%
where the time goes in v7:
time: 102 us; the launch traced here: 101 us
  blocking collectives  40.8 us (40%)
  starting transfers between devices  23.7 us (23%)
  local copies, waits for them, and re-layouts  13.8 us (14%)
  Pallas kernels  10.7 us (10%)
  waiting for transfers between devices  8.34 us (8%)
  other arithmetic  2.88 us (3%)
    all_to_all x1, blocking collectives, local(): lax.all_to_all(part.reshape(replicas, chunk, width), 'replica', split_axi...  19 us
    all_to_all x1, starting transfers between devices, local(): got = lax.all_to_all(send, 'shard', split_axis=0, concat_axis=0, tiled=True)  18.9 us
    all_gather x1, blocking collectives, local(): every = lax.all_gather(updated, 'replica', axis=0, tiled=True)  16.3 us
    all_gather x1, blocking collectives, local(): lax.all_gather(theirs, 'replica', axis=0, tiled=True, axis_index_groups=p...  5.52 us
    gather x1, local copies, waits for them, and re-layouts, local(): values = jnp.take(table, turned, axis=0, mode='clip')  5.32 us
    all_to_all x1, waiting for transfers between devices, local(): got = lax.all_to_all(send, 'shard', split_axis=0, concat_axis=0, tiled=True)  5.17 us
    all_to_all x1, starting transfers between devices, local(): lax.all_to_all(picked, 'shard', split_axis=0, concat_axis=0, tiled=True)  4.86 us
    scatter x1, local copies, waits for them, and re-layouts, local(): jnp.zeros(row_state.shape, f32).at[touched_rows]  4.33 us
  transfers between devices with their start and end apart: 2, of which 2 were waited for; matrix products, arithmetic and copies ran while one was open for 14% of the time, Pallas kernels for 5%

profile of v7, /device:TPU:1, one launch (start us, length us, event | category | flops | bytes accessed | tf_op | source)
XLA Modules:
  0.0 101.1 jit_solution(14451380680068692390)
XLA Ops:
  0.6 2.6 %prep.1 = bf16[48,21,2,128]{3,2,1,0:T(2,128)(2,1)} custom-call(s32[20,1,48]{2,1,0:T(1,128)} %bitcast.21, s32[20,1,48]{2,1,0:T(1,128)} %bitcast.16, s32[1,48]{1,0:T(1,128)} %counts_ref.3, f32[40,256]{1,0:T(8,128)} %grad_ref.1), custom_call_target="tpu_custom_call" | custom-call | tf_op jit(solution)/shard_map/prep/pallas_call | solution.py:99
  3.3 18.9 %all-to-all-start = ((bf16[48,21,2,128]{3,2,1,0:T(2,128)(2,1)}), bf16[48,21,2,128]{3,2,1,0:T(2,128)(2,1)S(1)}, u32[]{:S(2)}, u32[]{:S(2)}) async-start(bf16[48,21,2,128]{3,2,1,0:T(2,128)(2,1)} %prep.1), calls=%async_computation | async-start | bytes 1032192 | tf_op jit(solution)/shard_map/all_to_all | solution.py:403
  22.2 0.7 copy-done.3
  22.9 0.7 copy-done.4
  23.5 0.4 member.1.member_ref
  24.0 0.8 copy-done
  24.7 0.2 copy.13.column_ref
  25.0 1.0 %sort.1.listed_ref = s32[1,1024]{1,0:T(1,128)S(1)} custom-call(f32[1,1024]{1,0:T(1,128)S(1)} %bitcast.19, f32[1024,1]{1,0:T(8,128)S(1)} %copy.13.column_ref), custom_call_target="tpu_custom_call" | custom-call | tf_op jit(solution)/shard_map/sort/pallas_call | solution.py:176
  26.0 0.5 broadcast.31
  26.5 0.7 reduce.3
  27.4 5.3 %gather_fusion = bf16[1024,256]{1,0:T(8,128)(2,1)S(1)} fusion(bf16[4096,256]{1,0:T(8,128)(2,1)} %param.7, s32[1024]{0:T(1024)S(1)} %get-tuple-element.41), kind=kCustom, calls=%fused_computation | custom fusion | bytes 1052672 | tf_op jit(solution)/shard_map/jit(_take)/gather | solution.py:416
  32.7 0.8 gather_fusion.1
  33.5 4.3 %scatter_custom_fusion = f32[4096]{0:T(1024)S(1)} fusion(s32[1024]{0:T(1024)S(1)} %get-tuple-element.39, f32[1024]{0:T(1024)S(1)} %broadcast.15, f32[]{:T(128)} %constant.9.clone.1), kind=kCustom, calls=%fused_computation.10 | custom fusion | bytes 16388 | tf_op jit(solution)/shard_map/scatter | solution.py:427
  38.1 1.9 %broadcast_select_fusion.table_ref = bf16[4096,256]{1,0:T(8,128)(2,1)S(1)} fusion(bf16[4096,256]{1,0:T(8,128)(2,1)} %param.7, pred[4096]{0:T(1024)(128)(4,1)S(1)} %get-tuple-element.36), kind=kLoop, calls=%fused_computation.3 | loop fusion | flops 1048576 | bytes 4198400 | tf_op jit(solution)/shard_map/jit(_where)/select_n | solution.py:431
  40.0 5.2 %all-to-all-done.got_ref = bf16[48,21,2,128]{3,2,1,0:T(2,128)(2,1)S(1)} async-done(((bf16[48,21,2,128]{3,2,1,0:T(2,128)(2,1)}), bf16[48,21,2,128]{3,2,1,0:T(2,128)(2,1)S(1)}, u32[]{:S(2)}, u32[]{:S(2)}) %all-to-all-start) | async-done | bytes 516128 | tf_op jit(solution)/shard_map/all_to_all | solution.py:403
  45.4 2.1 %hits.1 = (bf16[512,256]{1,0:T(8,128)(2,1)S(1)}, f32[512,256]{1,0:T(8,128)S(1)}, bf16[48,40,128]{2,1,0:T(8,128)(2,1)S(1)}) custom-call(bf16[48,21,2,128]{3,2,1,0:T(2,128)(2,1)S(1)} %all-to-all-done.got_ref, f32[1024,128]{1,0:T(8,128)S(1)} %broadcast_in_dim.37.column_ref, bf16[1024,256]{1,0:T(8,128)(2,1)S(1)} %gather_fusion), custom_call_target="tpu_custom_call" | custom-call | tf_op jit(solution)/shard_map/hits/pallas_call | solution.py:234
  47.5 5.5 %all_gather.6 = bf16[1024,256]{1,0:T(8,128)(2,1)S(1)} all-gather(bf16[512,256]{1,0:T(8,128)(2,1)S(1)} %get-tuple-element.25), channel_id=1, replica_groups={{0,48},{96,144},{192,240},{288,336},{384,432},{480,528},{576,624},{672,..., dimensions={0}, use_global_device_ids=true | all-gather | bytes 786432 | tf_op jit(solution)/shard_map/all_gather | solution.py:441
  53.1 19.0 %all_to_all.15.parts_ref = bf16[16,32,256]{2,1,0:T(8,128)(2,1)S(1)} all-to-all(bf16[16,32,256]{2,1,0:T(8,128)(2,1)S(1)} %bitcast.20), channel_id=1, replica_groups=mesh['replica'=16,'shard'=48] {'replica'}, dimensions={0} | all-to-all | bytes 524288 | tf_op jit(solution)/shard_map/all_to_all | solution.py:444
  72.1 4.9 %all-to-all-start.2 = ((bf16[48,40,128]{2,1,0:T(8,128)(2,1)}), bf16[48,40,128]{2,1,0:T(8,128)(2,1)S(1)}, u32[]{:S(2)}, u32[]{:S(2)}) async-start(bf16[48,40,128]{2,1,0:T(8,128)(2,1)} %copy-done.2), calls=%async_computation.2 | async-start | bytes 983040 | tf_op jit(solution)/shard_map/all_to_all | solution.py:449
  77.1 0.2 update.1
  77.3 16.3 %all_gather.7.every_ref = bf16[1280,256]{1,0:T(8,128)(2,1)S(1)} all-gather(bf16[80,256]{1,0:T(8,128)(2,1)S(1)} %update.1), channel_id=1, replica_groups=mesh['replica'=16,'shard'=48] {'replica'}, dimensions={0}, use_global_device_ids=true | all-gather | bytes 696320 | tf_op jit(solution)/shard_map/all_gather | solution.py:451
  93.6 3.4 %place.1 = (bf16[4096,256]{1,0:T(8,128)(2,1)}, f32[32,128]{1,0:T(8,128)}) custom-call(s32[32]{0:T(128)S(1)} %convert_reduce_fusion.starts, bf16[1280,256]{1,0:T(8,128)(2,1)S(1)} %all_gather.7.every_ref, s32[1,1024]{1,0:T(1,128)S(1)} %sort.1.listed_ref, s32[16,128]{1,0:T(8,128)S(1)} %pad.4.tiles_ref, bf16[4096,256]{1,0:T(8,128)(2,1)S(1)} %broadcast_select_fusion.table_ref, ...), custom_call_target="tpu_custom_call" | custom-call | tf_op jit(solution)/shard_map/place/pallas_call | solution.py:349
  97.0 3.2 %all-to-all-done.2 = bf16[48,40,128]{2,1,0:T(8,128)(2,1)S(1)} async-done(((bf16[48,40,128]{2,1,0:T(8,128)(2,1)}), bf16[48,40,128]{2,1,0:T(8,128)(2,1)S(1)}, u32[]{:S(2)}, u32[]{:S(2)}) %all-to-all-start.2) | async-done | bytes 491552 | tf_op jit(solution)/shard_map/all_to_all | solution.py:449
  100.2 0.9 pool.1
  (28 shorter events, 0.8 us)
Async XLA Ops:
  0.6 24.1 %copy-start.6 = (s32[1024]{0:T(1024)S(1)}, s32[1024]{0:T(1024)}, u32[]{:S(2)}) copy-start(s32[1024]{0:T(1024)} %param.9) | copy-start | bytes 12292
  3.3 41.9 %all-to-all-start = ((bf16[48,21,2,128]{3,2,1,0:T(2,128)(2,1)}), bf16[48,21,2,128]{3,2,1,0:T(2,128)(2,1)S(1)}, u32[]{:S(2)}, u32[]{:S(2)}) async-start(bf16[48,21,2,128]{3,2,1,0:T(2,128)(2,1)} %prep.1), calls=%async_computation | async-start | bytes 1032192 | tf_op jit(solution)/shard_map/all_to_all | solution.py:403
  22.2 0.7 copy-start.3
  22.9 0.7 copy-start.4
  23.9 0.8 copy-start
  27.4 5.3 %copy-start.5 = (f32[4096]{0:T(1024)S(1)}, f32[4096]{0:T(1024)}, u32[]{:S(2)}) copy-start(f32[4096]{0:T(1024)} %param.8) | copy-start | bytes 49156
  47.5 24.6 %copy-start.2 = (bf16[48,40,128]{2,1,0:T(8,128)(2,1)}, bf16[48,40,128]{2,1,0:T(8,128)(2,1)S(1)}, u32[]{:S(2)}) copy-start(bf16[48,40,128]{2,1,0:T(8,128)(2,1)S(1)} %get-tuple-element.26) | copy-start | bytes 1474564
  72.1 28.1 %all-to-all-start.2 = ((bf16[48,40,128]{2,1,0:T(8,128)(2,1)}), bf16[48,40,128]{2,1,0:T(8,128)(2,1)S(1)}, u32[]{:S(2)}, u32[]{:S(2)}) async-start(bf16[48,40,128]{2,1,0:T(8,128)(2,1)} %copy-done.2), calls=%async_computation.2 | async-start | bytes 983040 | tf_op jit(solution)/shard_map/all_to_all | solution.py:449
  77.0 23.2 %copy-start.1 = (bf16[128,1920]{1,0:T(8,128)(2,1)S(1)}, bf16[128,1920]{1,0:T(8,128)(2,1)}, u32[]{:S(2)}) copy-start(bf16[128,1920]{1,0:T(8,128)(2,1)} %copy-done) | copy-start | bytes 1474564
